TPU v7x, 128 devices: a whole 4x4x4 slice. The times are simulated.
128 devices in a mesh: segment: 2 (over core), fsdp: 32 (over x, y_lo, z), dp: 2 (over y_hi).
Axes of the slice: x: 4, y: 4 (y_hi: 2, y_lo: 2; y = y_hi * 2 + y_lo), z: 4, core: 2. Of those that a mesh axis runs over, the one named last changes fastest.
Arguments:
- hooks: bfloat16 [2, 4, 256, 64, 6144], P('segment', 'dp', 'fsdp'), may hold values from -6 to 6
- proj_weight: bfloat16 [2, 6144, 256], P('segment', 'fsdp'), may hold values from -0.078125 to 0.078125
- conv_weight: bfloat16 [2, 2, 2304, 256], P('segment', None, 'fsdp'), may hold values from -0.125 to 0.125
- head_weight: bfloat16 [3, 256], replicated, may hold values from -0.375 to 0.375
- light_color: float32 [25, 3], replicated, may hold values from 0.3 to 1.5
- illum: int32 [4, 4], P('dp'), may hold values from 0 to 24
- offsets: int32 [4, 4, 2], P('dp'), may hold values from 0 to 32
- photos: bfloat16 [4, 4, 3, 96, 96], P('dp'), may hold values from 0 to 10
Outputs:
- grad_proj: float32 [2, 6144, 256], P('segment', 'fsdp')
- grad_conv: float32 [2, 2, 2304, 256], P('segment', None, 'fsdp')
- grad_head: float32 [3, 256], replicated
- loss: float32 [], replicated
All inputs are finite; a program needn't handle non-finite values.
Results may differ from a plain program's by a relative error of at most 0.018.
Values may be sent and summed in bfloat16 or wider, within the bound.
A program may use at most 128 MiB of HBM per device.

v0:
```python
import jax
import jax.numpy as jnp
from jax import lax
from jax.sharding import PartitionSpec as P

LOSS_SCALE = 8192.0


def extended(shard, sides, width):
    for axis, dim in sides:
        size, length = (lax.axis_size(axis), shard.shape[dim])
        up = [(i, (i + 1) % size) for i in range(size - 1)]
        down = [(j, i) for i, j in up]
        last = lax.slice_in_dim(shard, length - width, length, axis=dim)
        initial = lax.slice_in_dim(shard, 0, width, axis=dim)
        before = lax.ppermute(last, axis, up)
        after = lax.ppermute(initial, axis, down)
        shard = jnp.concatenate([before, shard, after], axis=dim)
    return shard


def shifted(shard, axis, by):
    size = lax.axis_size(axis)
    pairs = [(i, i + by) for i in range(size) if 0 <= i + by < size]
    return lax.ppermute(shard, axis, pairs)


def activate(values):
    return jax.nn.gelu(values, approximate=True)


def activate_slope(values):
    return jax.vjp(activate, values)[1](jnp.ones_like(values))[0]


def patches(field):
    rows_here, cols_here, channels = (field.shape[1], field.shape[2], field.shape[3])
    padded = extended(field, (("fsdp", 1),), 1)
    row_base = lax.axis_index("fsdp") * rows_here % cols_here
    upper = jnp.where(row_base == 0, jnp.zeros_like(padded[:, :1]), padded[:, :1])
    lower = jnp.where(
        row_base + rows_here == cols_here, jnp.zeros_like(padded[:, -1:]), padded[:, -1:]
    )
    padded = jnp.concatenate([upper, padded[:, 1:-1], lower], axis=1)
    padded = jnp.pad(padded, ((0, 0), (0, 0), (1, 1), (0, 0)))
    pieces = [
        padded[:, i : i + rows_here, j : j + cols_here, :] for i in range(3) for j in range(3)
    ]
    return jnp.concatenate(pieces, axis=-1).reshape(-1, 9 * channels)


def contract_rows(left, right):
    return lax.dot_general(
        left, right, (((0,), (0,)), ((), ())), preferred_element_type=jnp.float32
    )


def flipped(kernel):
    channels = kernel.shape[1]
    grid_form = kernel.reshape(3, 3, channels, channels)[::-1, ::-1]
    return jnp.swapaxes(grid_form, 2, 3).reshape(9 * channels, channels)


def section_parts(segment_in, first_conv, second_conv):
    channels = segment_in.shape[-1]
    first_in = activate(segment_in.astype(jnp.float32)).astype(jnp.bfloat16)
    first_patches = patches(first_in)
    hidden = jnp.dot(first_patches, first_conv, preferred_element_type=jnp.float32)
    second_in = activate(hidden).astype(jnp.bfloat16).reshape(segment_in.shape)
    second_patches = patches(second_in)
    update = jnp.dot(second_patches, second_conv, preferred_element_type=jnp.float32)
    output = (segment_in.reshape(-1, channels).astype(jnp.float32) + update).astype(jnp.bfloat16)
    return (output.reshape(segment_in.shape), first_patches, hidden, second_patches)


def section_back(segment_in, out_grad, first_conv, second_conv, first_flip, second_flip):
    channels = segment_in.shape[-1]
    output, first_patches, hidden, second_patches = section_parts(
        segment_in, first_conv, second_conv
    )
    out_rows = out_grad.reshape(-1, channels)
    second_grad = jnp.dot(patches(out_grad), second_flip, preferred_element_type=jnp.float32)
    hidden_grad = (second_grad * activate_slope(hidden)).astype(jnp.bfloat16)
    first_grad = jnp.dot(
        patches(hidden_grad.reshape(segment_in.shape)),
        first_flip,
        preferred_element_type=jnp.float32,
    )
    slope = activate_slope(segment_in.reshape(-1, channels).astype(jnp.float32))
    in_grad = (
        (out_rows.astype(jnp.float32) + first_grad * slope)
        .astype(jnp.bfloat16)
        .reshape(segment_in.shape)
    )
    return (
        in_grad,
        contract_rows(first_patches, hidden_grad),
        contract_rows(second_patches, out_rows),
    )


def head_loss(output, head_weight, tints, targets, factor):
    channels = output.shape[-1]
    out_rows = output.reshape(-1, channels)
    logits = lax.dot_general(
        head_weight, out_rows, (((1,), (1,)), ((), ())), preferred_element_type=jnp.float32
    )
    albedo = jax.nn.sigmoid(logits.reshape(targets.shape))
    tint = jnp.transpose(tints)[:, :, None, None]
    mismatch = albedo * tint - targets
    squares = jnp.sum(mismatch * mismatch)
    logit_grad = (
        (factor * mismatch * tint * albedo * (1.0 - albedo)).astype(jnp.bfloat16).reshape(3, -1)
    )
    head_grad = lax.dot_general(
        logit_grad, out_rows, (((1,), (0,)), ((), ())), preferred_element_type=jnp.float32
    )
    out_grad = lax.dot_general(
        logit_grad, head_weight, (((0,), (0,)), ((), ())), preferred_element_type=jnp.float32
    )
    return (squares, head_grad, out_grad.astype(jnp.bfloat16).reshape(output.shape))


def crop_tints(illum, light_color):
    lights = light_color.shape[0]
    onehot = (illum[..., None] == jnp.arange(lights, dtype=jnp.int32)).astype(jnp.float32)
    return jnp.dot(onehot.reshape(-1, lights), light_color, precision=lax.Precision.HIGHEST)


def crop_targets(photos, offsets, row_base, rows_here, cols_here):

    def one_crop(picture, offset):
        start = (jnp.zeros((), jnp.int32), offset[0] + row_base, offset[1])
        return lax.dynamic_slice(picture, start, (3, rows_here, cols_here))

    cut = jax.vmap(jax.vmap(one_crop))(photos, offsets).astype(jnp.float32)
    return jnp.moveaxis(cut, 2, 0)


def fetch_convs(conv_weight):
    gathered = lax.all_gather(conv_weight[0], "fsdp", axis=1, tiled=True)
    return (gathered[0], gathered[1])


def pass_on(field):
    return shifted(field, "segment", 1)


def pass_back(field):
    return shifted(field, "segment", -1)


def body(hooks, proj_weight, conv_weight, head_weight, light_color, illum, offsets, photos):
    segments = lax.axis_size("segment")
    segment_index = lax.axis_index("segment")
    is_last = segment_index == segments - 1
    micro_count, band_rows, grid_cols, model_width = (
        hooks.shape[1],
        hooks.shape[2],
        hooks.shape[3],
        hooks.shape[4],
    )
    crop_count = 1
    channels = proj_weight.shape[2]
    tokens = hooks[0].reshape(-1, model_width)
    first_global = lax.axis_index("fsdp") * band_rows
    crop_here = first_global // grid_cols
    row_base = first_global % grid_cols
    columns = tokens
    projected = jnp.dot(
        columns,
        lax.all_gather(proj_weight[0], "fsdp", axis=0, tiled=True),
        preferred_element_type=jnp.float32,
    )
    projected = projected.astype(jnp.bfloat16).reshape(
        micro_count, crop_count, band_rows, grid_cols, channels
    )
    first_conv, second_conv = fetch_convs(conv_weight)
    micro_shape = (crop_count, band_rows, grid_cols, channels)
    flat_shape = (micro_count * crop_count, band_rows, grid_cols, channels)
    flat_proj = projected.reshape(flat_shape)
    incoming = jnp.zeros_like(flat_proj)
    for p in range(segments):
        segment_in = (flat_proj.astype(jnp.float32) + incoming.astype(jnp.float32)).astype(
            jnp.bfloat16
        )
        output = section_parts(segment_in, first_conv, second_conv)[0]
        if p + 1 < segments:
            incoming = pass_on(output)
    inputs_all = segment_in.reshape((micro_count,) + micro_shape)
    outputs_all = output.reshape((micro_count,) + micro_shape)
    illum_here = lax.dynamic_slice_in_dim(illum, crop_here, 1, 1)
    offsets_here = lax.dynamic_slice_in_dim(offsets, crop_here, 1, 1)
    photos_here = lax.dynamic_slice_in_dim(photos, crop_here, 1, 1)
    tints = crop_tints(illum_here, light_color)
    targets = crop_targets(photos_here, offsets_here, row_base, band_rows, grid_cols)
    targets = targets.reshape(3, micro_count * crop_count, band_rows, grid_cols)
    npix = 3 * micro_count * lax.axis_size("dp") * band_rows * lax.axis_size("fsdp") * grid_cols
    factor = 2.0 * LOSS_SCALE / npix
    squares, head_grad, out_grads = head_loss(
        outputs_all.reshape(flat_shape), head_weight, tints, targets, factor
    )
    out_grads = out_grads.reshape((micro_count,) + micro_shape)
    back_first, back_second = fetch_convs(conv_weight)
    first_flip = flipped(back_first)
    second_flip = flipped(back_second)
    flat_in = inputs_all.reshape(flat_shape)
    flat_grads = out_grads.reshape(flat_shape)
    received = jnp.zeros_like(flat_grads)
    for p in range(segments):
        out_grad = jnp.where(is_last, flat_grads, received)
        in_grad, first_sum, second_sum = section_back(
            flat_in, out_grad, back_first, back_second, first_flip, second_flip
        )
        if p + 1 < segments:
            received = pass_back(in_grad)
    grad_rows = in_grad.reshape(-1, channels)
    conv_sums = jnp.concatenate([first_sum, second_sum], axis=1)
    columns = tokens
    proj_part = lax.psum_scatter(
        contract_rows(columns, grad_rows), "fsdp", scatter_dimension=0, tiled=True
    )
    conv_part = lax.psum_scatter(conv_sums, "fsdp", scatter_dimension=0, tiled=True)
    proj_part, conv_part = lax.psum((proj_part, conv_part), "dp")
    loss_term = jnp.where(is_last, squares, 0.0)
    head_term = jnp.where(is_last, head_grad, 0.0)
    head_total, square_total = lax.psum((head_term, loss_term), ("segment", "fsdp", "dp"))
    grad_conv = jnp.stack([conv_part[:, :channels], conv_part[:, channels:]])[None]
    return (proj_part[None], grad_conv, head_total, square_total / npix)


def solution(mesh):
    placed = (
        P("segment", "dp", "fsdp", None, None),
        P("segment", "fsdp", None),
        P("segment", None, "fsdp", None),
        P(),
        P(),
        P("dp", None),
        P("dp", None, None),
        P("dp", None, None, None, None),
    )
    return jax.shard_map(
        body,
        mesh=mesh,
        in_specs=placed,
        out_specs=(P("segment", "fsdp", None), P("segment", None, "fsdp", None), P(), P()),
        check_vma=False,
    )
```

profile of v0, /device:TPU:0, one launch (start us, length us, event | category | flops | bytes accessed | tf_op | source)
XLA Modules:
  0.0 881.8 jit_solution(2431889212769604529)
XLA Ops:
  9.6 158.0 %all-gather.5.cloned.1.call-done = bf16[1,6144,256]{2,1,0:T(8,128)(2,1)} async-done(((bf16[1,192,256]{2,1,0:T(8,128)(2,1)}), bf16[1,6144,256]{2,1,0:T(8,128)(2,1)}) %all-gather.5.cloned.1.call-update) | async-done | bytes 3145744 | tf_op jit(solution)/shard_map/all_gather | solution.py:172
  167.6 7.3 fusion.8
  175.3 1.3 collective-permute-start.1
  176.7 4.5 collective-permute-start
  181.5 1.7 collective-permute-done
  183.5 0.9 slice_dynamic-update-slice_fusion.23
  185.3 1.0 slice_dynamic-update-slice_fusion.22
  187.2 1.2 constant_dynamic-update-slice_fusion
  188.3 1.0 slice_dynamic-update-slice_fusion.20
  189.4 0.9 slice_dynamic-update-slice_fusion.19
  191.2 1.0 slice_dynamic-update-slice_fusion.18
  192.2 131.0 %all-gather.7.cloned.1.call-done = bf16[1,2,2304,256]{3,2,1,0:T(8,128)(2,1)} async-done(((bf16[1,2,72,256]{3,2,1,0:T(8,128)(2,1)}), bf16[1,2,2304,256]{3,2,1,0:T(8,128)(2,1)}) %all-gather.7.cloned.1.call-update) | async-done | bytes 2359312 | tf_op jit(solution)/shard_map/all_gather | solution.py:141
  323.1 4.2 fusion.54
  327.3 3.3 collective-permute-start.2
  330.7 1.3 collective-permute-start.3
  332.6 4.3 collective-permute-done.3
  338.3 1.3 copy-done.4
  339.5 1.4 fusion.11
  340.9 1.3 collective-permute-start.4
  342.5 12.9 %copy.50 = bf16[2,1,3,96,96]{2,1,0,4,3:T(2,128)(2,1)} copy(bf16[2,1,3,96,96]{4,3,2,1,0:T(8,128)(2,1)S(1)} %constant_dynamic-slice_fusion.2) | data formatting | bytes 221184
  355.3 3.3 gather_fusion
  360.5 1.8 collective-permute-start.5
  362.3 1.8 fusion.92
  364.1 1.8 collective-permute-start.6
  365.9 4.4 collective-permute-done.6
  372.2 2.5 multiply_convert_fusion
  374.7 1.9 collective-permute-start.7
  376.7 1.3 collective-permute-start.8
  378.5 4.3 collective-permute-done.8
  384.9 1.8 copy-done.12
  386.7 1.4 fusion.12
  389.6 1.3 collective-permute-start.10
  391.0 1.6 copy.40
  393.3 4.5 collective-permute-start.9
  398.7 1.3 collective-permute-done.9
  401.9 1.8 fusion.13
  403.7 4.2 collective-permute-start.11
  408.6 1.5 collective-permute-start.12
  410.1 4.7 collective-permute-done.12
  416.1 1.4 fusion.4
  417.5 1.3 collective-permute-start.13
  418.8 2.5 collective-permute-done.13
  421.4 5.2 collective-permute-start.14
  426.6 1.3 collective-permute-start.15
  427.9 1.5 convolution_bitcast_fusion.1
  429.4 5.7 collective-permute-done.15
  436.3 1.8 fusion.14
  438.4 1.5 fusion.104
  439.9 2.5 pad_maximum_fusion
  442.4 6.1 copy.48
  448.5 6.0 collective-permute-start.16
  454.6 1.5 collective-permute-start.17
  456.5 4.3 collective-permute-done.17
  462.1 2.2 copy-done.11
  464.3 16.0 %convolution_bitcast_fusion = f32[6144,256]{0,1:T(8,128)} fusion(bf16[1024,6144]{1,0:T(8,128)(2,1)} %bitcast.223, bf16[1024,256]{1,0:T(8,128)(2,1)S(1)} %bitcast.150, f32[1024,256]{1,0:T(8,128)S(1)} %fusion.36, bf16[1024,2304]{1,0:T(8,128)(2,1)} %copy-done.11, bf16[2304,256]{1,0:T(8,128)(2,1)S(1)} %bitcast.207), kind=kOutput, calls=%fused_computation.1 | convolution fusion | flops 4430233600 | bytes 26345472 | tf_op jit(solution)/shard_map/dot_general | solution.py:53
  480.3 6.6 copy.46
  487.3 139.7 %reduce-scatter.9.cloned.1.call-done = f32[72,512]{1,0:T(8,128)} async-done(((f32[2304,512]{1,0:T(8,128)}), f32[72,512]{1,0:T(8,128)}) %reduce-scatter.9.cloned.1.call-update) | async-done | bytes 147472
  627.0 1.7 copy.49
  628.7 171.5 %reduce-scatter.7.cloned.1.call-done = f32[192,256]{1,0:T(8,128)} async-done(((f32[6144,256]{1,0:T(8,128)}), f32[192,256]{1,0:T(8,128)}) %reduce-scatter.7.cloned.1.call-update) | async-done | bytes 196624
  800.2 1.8 copy.47
  802.0 1.1 fusion.73
  804.0 65.7 %all-reduce.8 = (f32[3,256]{1,0:T(4,128)}, f32[]{:T(128)}) all-reduce(f32[3,256]{1,0:T(4,128)S(1)} %convolution_select_fusion, f32[]{:T(128)S(6)} %select_n.191), channel_id=1, replica_groups=mesh['segment'=2,'fsdp'=32,'dp'=2] {'segment','fsdp','dp'}, use_global_device_ids=true, to_apply=%region_4.5 | all-reduce | flops 769 | bytes 6152 | tf_op jit(solution)/shard_map/psum | solution.py:227
  870.4 1.0 slice_bitcast_fusion.1
  872.2 1.7 copy.43
  (208 shorter events, 25.9 us)
Async XLA Ops:
  7.2 323.5 %copy-start = (bf16[2,4,3,96,96]{4,3,2,1,0:T(8,128)(2,1)S(1)}, bf16[2,4,3,96,96]{4,3,2,1,0:T(8,128)(2,1)}, u32[]{:S(2)}) copy-start(bf16[2,4,3,96,96]{4,3,2,1,0:T(8,128)(2,1)} %param.15) | copy-start | bytes 1327108
  7.2 160.4 %all-gather.5.cloned.1.call-start = ((), (), s32[]{:S(2)}) async-start(), calls=%async_computation.2 | async-start | bytes 3244032 | tf_op jit(solution)/shard_map/all_gather | solution.py:172
  7.9 315.2 %all-gather.7.cloned.1.call-start = ((), (), s32[]{:S(2)}) async-start(), calls=%async_computation.3 | async-start | bytes 2433024 | tf_op jit(solution)/shard_map/all_gather | solution.py:141
  8.7 618.3 %reduce-scatter.9.cloned.1.call-start = ((), (), s32[]{:S(2)}) async-start(), calls=%async_computation.5 | async-start | bytes 4866048
  175.3 6.2 collective-permute-start.1
  176.7 6.4 collective-permute-start
  327.3 5.2 collective-permute-start.2
  330.7 6.2 collective-permute-start.3
  337.8 1.7 copy-start.4
  340.9 19.1 %collective-permute-start.4 = (bf16[2,8,64,256]{3,2,1,0:T(8,128)(2,1)S(1)}, bf16[2,8,64,256]{3,2,1,0:T(8,128)(2,1)S(1)}, u32[]{:S(2)}, u32[]{:S(2)}) collective-permute-start(bf16[2,8,64,256]{3,2,1,0:T(8,128)(2,1)S(1)} %bitcast.224), channel_id=1, source_target_pairs={{0,64},{1,65},{2,66},{3,67},{4,68},{5,69},{6,70},{7,71},{8,72},{9,... | collective-permute-start | bytes 1572872 | tf_op jit(solution)/shard_map/ppermute | solution.py:25
  342.4 16.7 %copy-start.15 = (s32[2,4]{1,0:T(2,128)S(1)}, s32[2,4]{1,0:T(2,128)}, u32[]{:S(2)}) copy-start(s32[2,4]{1,0:T(2,128)} %param.13) | copy-start | bytes 100
  342.4 16.9 %copy-start.16 = (f32[25,3]{0,1:T(4,128)S(1)}, f32[25,3]{0,1:T(4,128)}, u32[]{:S(2)}) copy-start(f32[25,3]{0,1:T(4,128)} %param.12) | copy-start | bytes 904
  358.6 5.4 copy-start.9
  360.5 26.2 %copy-start.2 = (f32[2,8,64,256]{3,2,1,0:T(8,128)}, f32[2,8,64,256]{3,2,1,0:T(8,128)S(1)}, u32[]{:S(2)}) copy-start(f32[2,8,64,256]{3,2,1,0:T(8,128)S(1)} %get-tuple-element.29) | copy-start | bytes 3145732
  360.5 5.3 collective-permute-start.5
  364.1 6.2 collective-permute-start.6
  370.6 1.7 copy-start.5
  371.4 3.3 copy-start.13
  374.7 3.8 collective-permute-start.7
  376.7 6.2 collective-permute-start.8
  384.5 2.2 copy-start.12
  386.7 1.4 copy-start.14
  388.1 0.8 copy-start.6
  389.6 8.2 collective-permute-start.10
  393.3 6.8 collective-permute-start.9
  400.4 1.3 copy-start.8
  400.4 1.6 copy-start.17
  401.9 6.0 copy-start.3
  403.7 6.3 collective-permute-start.11
  408.6 6.2 collective-permute-start.12
  416.1 11.8 %slice-start = ((s8[4718592]{0:T(1024)(128)(4,1)}), s8[524288]{0:T(1024)(128)(4,1)S(1)}, s32[]{:S(2)}) async-start(s8[4718592]{0:T(1024)(128)(4,1)} %bitcast.211), calls=%async_computation.7 | async-start | bytes 1048576
  416.1 11.8 %slice-start.1 = ((s8[4718592]{0:T(1024)(128)(4,1)}), s8[4194304]{0:T(1024)(128)(4,1)S(1)}, s32[]{:S(2)}) async-start(s8[4718592]{0:T(1024)(128)(4,1)} %bitcast.211), calls=%async_computation.8 | async-start | bytes 8388608
  417.5 3.8 collective-permute-start.13
  421.4 8.0 collective-permute-start.14
  426.6 8.5 collective-permute-start.15
  436.0 2.2 slice-start.2
  436.3 2.1 slice-start.3
  448.5 351.8 %reduce-scatter.7.cloned.1.call-start = ((), (), s32[]{:S(2)}) async-start(), calls=%async_computation.4 | async-start | bytes 6488064
  448.5 7.9 collective-permute-start.16
  454.6 6.2 collective-permute-start.17
  462.1 2.2 copy-start.11
  486.8 315.2 %copy-start.10 = (bf16[2,3,8,64]{1,0,3,2:T(2,128)(2,1)S(1)}, bf16[2,3,8,64]{1,0,3,2:T(2,128)(2,1)}, u32[]{:S(2)}) copy-start(bf16[2,3,8,64]{1,0,3,2:T(2,128)(2,1)} %copy-done.9) | copy-start | bytes 18436
  486.8 317.0 %copy-start.7 = (bf16[1024,256]{1,0:T(8,128)(2,1)S(1)}, bf16[1024,256]{1,0:T(8,128)(2,1)}, u32[]{:S(2)}) copy-start(bf16[1024,256]{1,0:T(8,128)(2,1)} %copy-done.6) | copy-start | bytes 1572868
  486.8 387.1 %copy-start.1 = (bf16[2,4,3,96,96]{4,3,2,1,0:T(8,128)(2,1)S(1)}, bf16[2,4,3,96,96]{4,3,2,1,0:T(8,128)(2,1)}, u32[]{:S(2)}) copy-start(bf16[2,4,3,96,96]{4,3,2,1,0:T(8,128)(2,1)} %param.15) | copy-start | bytes 1327108
  486.9 383.5 %all-reduce.12.cloned.1.call-start = ((), (), s32[]{:S(2)}) async-start(), calls=%async_computation.6 | async-start | bytes 1048576 | tf_op jit(solution)/shard_map/psum | solution.py:224
Sparse Core Ops, SparseCore 0:
  9.7 157.8 all-gather.4
  169.2 153.8 all-gather.6
  448.6 178.3 reduce-scatter.8
  629.3 170.9 reduce-scatter.6
  802.6 33.2 all-reduce.11
where the time goes:
time: 890 us; the launch traced here: 882 us
  waiting for transfers between devices  636 us (71%)
  blocking collectives  65.7 us (7%)
  local copies, waits for them, and re-layouts  62.2 us (7%)
  starting transfers between devices  45.5 us (5%)
  matrix products  41.6 us (5%)
  between operations  17.8 us (2%)
  other arithmetic  12.8 us (1%)
    unnamed x7, waiting for transfers between devices  313 us
    all_gather x1, waiting for transfers between devices, body(): lax.all_gather(proj_weight[0], 'fsdp', axis=0, tiled=True)  158 us
    all_gather x1, waiting for transfers between devices, fetch_convs(): gathered = lax.all_gather(conv_weight[0], 'fsdp', axis=1, tiled=True)  131 us
    psum x1, blocking collectives, body(): lax.psum((head_term, loss_term), ('segment', 'fsdp', 'dp'))  65.7 us
    unnamed x114, local copies, waits for them, and re-layouts  46.8 us
    ppermute x8, starting transfers between devices, extended(): before = lax.ppermute(last, axis, up)  31.5 us
    ppermute x8, waiting for transfers between devices, extended(): after = lax.ppermute(initial, axis, down)  27.7 us
    dot_general x3, matrix products, contract_rows(): lax.dot_general(left, right, (((0,), (0,)), ((), ())), preferred_element_...  18.9 us
  transfers between devices with their start and end apart: 23, of which 17 were waited for; matrix products, arithmetic and copies ran while one was open for 8% of the time, Pallas kernels for 0%

commit v1 on v0

v1 whole, which is shorter than its diff:
```python
import functools

import jax
import jax.numpy as jnp
from jax import lax
from jax.experimental import pallas as pl
from jax.experimental.pallas import tpu as pltpu
from jax.sharding import PartitionSpec as P

LOSS_SCALE = 8192.0
MESH = pl.DeviceIdType.MESH
BF = jnp.bfloat16
F32 = jnp.float32

MICROS, ROWS, COLS, CH = 2, 8, 64, 256
TOKENS = MICROS * ROWS * COLS
HALF = ROWS * COLS
D = 6144
SLOT = 192
CSLOT = 72
CHUNK = 4 * SLOT

ORDER = [(0, 0), (0, 1), (-1, 0), (1, 0), (-1, 1), (1, 1), (2, 0), (2, 1)]
BACK = [(2, 0), (2, 1), (-1, 0), (1, 1), (1, 0), (-1, 1), (0, 1), (0, 0)]


def place():
    f = lax.axis_index("fsdp")
    return f // 8, (f // 4) % 2, f % 4


def at(x, y, z):
    return {"fsdp": x * 8 + y * 4 + z}


def dot(a, b, dims=((1,), (0,))):
    return lax.dot_general(a, b, (dims, ((), ())), preferred_element_type=F32)


def gelu_parts(v):
    c = 0.7978845608028654
    t = jnp.tanh(c * (v + 0.044715 * (v * v * v)))
    return t


def gelu(v):
    return 0.5 * v * (1.0 + gelu_parts(v))


def gelu_slope(v):
    c = 0.7978845608028654
    t = gelu_parts(v)
    return 0.5 * (1.0 + t) + 0.5 * v * (1.0 - t * t) * (c * (1.0 + 3.0 * 0.044715 * (v * v)))


class Axis:
    def __init__(self, p_is_x):
        x, y, z = place()
        self.p_is_x = p_is_x
        self.p, self.y, self.q = (x, y, z) if p_is_x else (z, y, x)

    def coords(self, dp, r, dq):
        p = (self.p + (dp + 4)) % 4
        q = (self.q + (dq + 4)) % 4
        y = (self.y + r) % 2
        return (p, y, q) if self.p_is_x else (q, y, p)

    def slot(self, dp, r, dq):
        x, y, z = self.coords(dp, r, dq)
        return x * 8 + y * 4 + z

    def device(self, dp, r, dq):
        return at(*self.coords(dp, r, dq))


def rel(dp, r, dq):
    return ((dp % 4) * 2 + r) * 4 + dq % 4


class Gather:
    def __init__(self, axis, buf, send, recv):
        self.a, self.buf, self.send, self.recv = axis, buf, send, recv
        self.copies = []

    def put(self, dp, r, dq, to):
        tp, tr, tq = to
        a = self.a
        slot = a.slot(dp, r, dq)
        copy = pltpu.make_async_remote_copy(
            src_ref=self.buf.at[slot],
            dst_ref=self.buf.at[slot],
            send_sem=self.send.at[len(self.copies)],
            recv_sem=self.recv.at[rel(dp - tp, (r + tr) % 2, dq - tq)],
            device_id=a.device(tp, tr, tq),
            device_id_type=MESH,
        )
        copy.start()
        self.copies.append(copy)

    def await_(self, dp, r, dq):
        a = self.a
        slot = a.slot(dp, r, dq)
        pltpu.make_async_remote_copy(
            src_ref=self.buf.at[slot],
            dst_ref=self.buf.at[slot],
            send_sem=self.send.at[0],
            recv_sem=self.recv.at[rel(dp, r, dq)],
            device_id=a.device(0, 1, 0),
            device_id_type=MESH,
        ).wait_recv()

    def event(self, i):
        dp, r = ORDER[i]
        if i > 0:
            self.await_(dp, r, 0)
        if i == 0:
            self.put(0, 0, 0, (0, 1, 0))
        if dp == 0:
            self.put(0, r, 0, (1, 0, 0))
            self.put(0, r, 0, (-1, 0, 0))
        if (dp, r) == (-1, 0):
            self.put(dp, r, 0, (1, 0, 0))
        if (dp, r) == (1, 1):
            self.put(dp, r, 0, (-1, 0, 0))
        self.put(dp, r, 0, (0, 0, 1))
        self.put(dp, r, 0, (0, 0, -1))

    def onward(self, i):
        dp, r = ORDER[i]
        self.await_(dp, r, -1)
        if r == 0:
            self.put(dp, r, -1, (0, 0, 1))
        self.await_(dp, r, 1)
        if r == 1:
            self.put(dp, r, 1, (0, 0, -1))

    def last(self, i):
        dp, r = ORDER[i]
        self.await_(dp, r, 2)

    def drain(self):
        for copy in self.copies:
            copy.wait_send()


def entry_barrier(devices):
    barrier = pltpu.get_barrier_semaphore()
    for device in devices:
        pl.semaphore_signal(barrier, inc=1, device_id=device, device_id_type=MESH)
    pl.semaphore_wait(barrier, len(devices))


def shift_parts(v):
    n = v.shape[0]
    col = lax.broadcasted_iota(jnp.int32, v.shape, 0) % COLS
    before = jnp.where(col == 0, 0.0, pltpu.roll(v, 1, 0))
    after = jnp.where(col == COLS - 1, 0.0, pltpu.roll(v, n - 1, 0))
    return before.astype(BF), v.astype(BF), after.astype(BF)


def main_kernel(
    npix,
    factor,
    hooks_ref,
    proj_ref,
    conv_ref,
    head_ref,
    light_ref,
    illum_ref,
    offsets_ref,
    photos_ref,
    grad_ref,
    gconv_ref,
    total_ref,
    hooks_v,
    wproj,
    wconv,
    wf32,
    wbf,
    acc,
    section_in,
    inc,
    out,
    og_in,
    og,
    hidden,
    cat_a,
    cat_b,
    cat_c,
    x1t,
    x2t,
    hsend,
    hrecv,
    targets,
    head_pad,
    hsum,
    hgot,
    hfin,
    load_sem,
    psend,
    precv,
    csend,
    crecv,
    hs_sem,
    hr_sem,
    seg_s,
    seg_r,
    sum_s,
    sum_r,
):
    x, y, z = place()
    seg = lax.axis_index("segment")
    dpi = lax.axis_index("dp")
    band = y * 4 + z
    sibling = {"segment": 1 - seg}
    dp_peer = {"dp": 1 - dpi}
    up_j, down_j = (band + 7) % 8, (band + 1) % 8
    up = at(x, up_j // 4, up_j % 4)
    down = at(x, down_j // 4, down_j % 4)

    loads = []
    pa = Axis(True)
    for i, (dp, r) in enumerate(ORDER):
        xs, ys, _ = pa.coords(dp, r, 0)
        c = xs * 2 + ys
        start = pl.multiple_of(c * CHUNK, CHUNK)
        copy = pltpu.make_async_copy(
            hooks_ref.at[:, pl.ds(start, CHUNK)], hooks_v.at[i], load_sem.at[i]
        )
        copy.start()
        loads.append(copy)

    me = x * 8 + y * 4 + z
    wproj[me] = proj_ref[...]
    wconv[me] = conv_ref[...]

    z1 = at(x, y, z + 1 - 2 * (z % 2))
    z2 = at(x, y, (z + 2) % 4)
    x1 = at(x + 1 - 2 * (x % 2), y, z)
    x2 = at((x + 2) % 4, y, z)
    y1 = at(x, 1 - y, z)
    entry_barrier(
        [
            at((x + 1) % 4, y, z),
            at((x + 3) % 4, y, z),
            at(x, y, (z + 1) % 4),
            at(x, y, (z + 3) % 4),
            y1,
            z2,
            x2,
            up,
            down,
            sibling,
            dp_peer,
        ]
    )

    gp = Gather(pa, wproj, psend, precv)
    gc = Gather(Axis(False), wconv, csend, crecv)

    gp.event(0)
    gc.event(0)

    yy = lax.broadcasted_iota(jnp.int32, (96, HALF), 0)
    nn = lax.broadcasted_iota(jnp.int32, (96, HALF), 1)
    row8 = lax.broadcasted_iota(jnp.int32, (8, HALF), 0)
    for m in range(MICROS):
        oy = offsets_ref[m, x, 0]
        ox = offsets_ref[m, x, 1]
        pick_col = (yy == ox + nn % COLS).astype(F32).astype(BF)
        pick_row = yy == oy + band * ROWS + nn // COLS
        block = jnp.zeros((8, HALF), F32)
        for c in range(3):
            q = dot(photos_ref[m, x, c], pick_col)
            line = jnp.sum(jnp.where(pick_row, q, 0.0), axis=0, keepdims=True)
            block = jnp.where(row8 == c, line, block)
        targets[:, m * HALF : (m + 1) * HALF] = block
    head_pad[...] = jnp.zeros((8, CH), F32)
    head_pad[0:3, :] = head_ref[...].astype(F32)

    acc[...] = jnp.zeros_like(acc)

    def project(i):
        loads[i].wait()
        dp, r = ORDER[i]
        xs, ys, _ = pa.coords(dp, r, 0)
        base = xs * 8 + ys * 4
        w = wproj[pl.ds(base, 4)].reshape(CHUNK, CH)

        def step(t, _):
            rows = pl.ds(pl.multiple_of(t * 256, 256), 256)
            acc[rows, :] += dot(hooks_v[i, rows, :], w)
            return 0

        lax.fori_loop(0, TOKENS // 256, step, 0)

    for i in range(1, 8):
        gp.event(i)
        gc.event(i)
        gp.onward(i - 1)
        gc.onward(i - 1)
        if i >= 2:
            gp.last(i - 2)
            gc.last(i - 2)
            project(i - 2)
    gp.onward(7)
    gc.onward(7)
    gc.last(6)
    gc.last(7)

    def gather_rows(k, _):
        start = pl.multiple_of(k * CSLOT, 8)
        wf32[0, pl.ds(start, CSLOT), :] = wconv[k, 0].astype(F32)
        wf32[1, pl.ds(start, CSLOT), :] = wconv[k, 1].astype(F32)
        return 0

    lax.fori_loop(0, 32, gather_rows, 0)

    def to_bf(k, _):
        start = pl.multiple_of(k * CH, CH)
        wbf[0, pl.ds(start, CH), :] = wf32[0, pl.ds(start, CH), :].astype(BF)
        wbf[1, pl.ds(start, CH), :] = wf32[1, pl.ds(start, CH), :].astype(BF)
        return 0

    lax.fori_loop(0, 9, to_bf, 0)
    gp.last(6)
    project(6)
    gp.last(7)
    project(7)
    gp.drain()
    gc.drain()

    def seg_copy(src, dst, k):
        return pltpu.make_async_remote_copy(
            src_ref=src,
            dst_ref=dst,
            send_sem=seg_s.at[k],
            recv_sem=seg_r.at[k],
            device_id=sibling,
            device_id_type=MESH,
        )

    @pl.when(seg == 0)
    def _():
        section_in[...] = acc[...].astype(BF)

    @pl.when(seg == 1)
    def _():
        seg_copy(out, inc, 0).wait_recv()
        section_in[...] = (acc[...].astype(BF).astype(F32) + inc[...].astype(F32)).astype(BF)

    halo_copies = []

    def halo_start(e):
        pair = []
        for side, device in ((0, up), (1, down)):
            copy = pltpu.make_async_remote_copy(
                src_ref=hsend.at[e, side],
                dst_ref=hrecv.at[e, 1 - side],
                send_sem=hs_sem.at[e, side],
                recv_sem=hr_sem.at[e, 1 - side],
                device_id=device,
                device_id_type=MESH,
            )
            copy.start()
            pair.append(copy)
        halo_copies.extend(pair)

    def fill(cat, m, value):
        a, b, c = shift_parts(value)
        shape = (ROWS, COLS, CH)
        cat[m, 1 : 1 + ROWS, :, 0:CH] = a.reshape(shape)
        cat[m, 1 : 1 + ROWS, :, CH : 2 * CH] = b.reshape(shape)
        cat[m, 1 : 1 + ROWS, :, 2 * CH : 3 * CH] = c.reshape(shape)

    def edges(e, m, value):
        hsend[e, 0, m] = value[0:COLS].astype(BF)
        hsend[e, 1, m] = value[HALF - COLS : HALF].astype(BF)

    def halo_wait(e, cat):
        for copy in halo_copies[-2:]:
            copy.wait()
        for side, row, last in ((0, 0, 0), (1, ROWS + 1, 7)):
            for m in range(MICROS):
                v = hrecv[e, side, m].astype(F32)
                v = jnp.where(band == last, jnp.zeros_like(v), v)
                a, b, c = shift_parts(v)
                cat[m, row, :, 0:CH] = a
                cat[m, row, :, CH : 2 * CH] = b
                cat[m, row, :, 2 * CH : 3 * CH] = c

    def tokens_of(m):
        return slice(m * HALF, (m + 1) * HALF)

    def conv(cat, which, m):
        total = None
        for ky in range(3):
            left = cat[m, ky : ky + ROWS].reshape(HALF, 3 * CH)
            part = dot(left, wbf[which, ky * 3 * CH : (ky + 1) * 3 * CH, :])
            total = part if total is None else total + part
        return total

    def conv_back(cat, which, m):
        total = None
        for ky in range(3):
            for kx in range(3):
                left = cat[m, ky : ky + ROWS, :, kx * CH : (kx + 1) * CH].reshape(HALF, CH)
                k = (2 - ky) * 3 + 2 - kx
                part = dot(left, wbf[which, k * CH : (k + 1) * CH, :], ((1,), (1,)))
                total = part if total is None else total + part
        return total

    def conv_weight_grad(xt, cat, which):
        for ky in range(3):
            total = None
            for m in range(MICROS):
                right = cat[m, 2 - ky : 2 - ky + ROWS].reshape(HALF, 3 * CH)
                part = dot(xt[:, tokens_of(m)], right)
                total = part if total is None else total + part
            for kx in range(3):
                j = 2 - kx
                row = (3 * ky + kx) * CH
                gconv_ref[which, row : row + CH, :] = total[:, j * CH : (j + 1) * CH]

    for m in range(MICROS):
        first = gelu(section_in[tokens_of(m), :].astype(F32)).astype(BF).astype(F32)
        edges(0, m, first)
        fill(cat_a, m, first)
    halo_start(0)
    for m in range(MICROS):
        first = cat_a[m, 1 : 1 + ROWS, :, CH : 2 * CH].reshape(HALF, CH).astype(F32)
        x1t[:, tokens_of(m)] = first.T.astype(BF)
    halo_wait(0, cat_a)
    for m in range(MICROS):
        h = conv(cat_a, 0, m)
        hidden[tokens_of(m), :] = h
        second = gelu(h).astype(BF).astype(F32)
        edges(1, m, second)
        fill(cat_b, m, second)
    halo_start(1)
    for m in range(MICROS):
        second = cat_b[m, 1 : 1 + ROWS, :, CH : 2 * CH].reshape(HALF, CH).astype(F32)
        x2t[:, tokens_of(m)] = second.T.astype(BF)
    halo_wait(1, cat_b)
    for m in range(MICROS):
        update = conv(cat_b, 1, m)
        out[tokens_of(m), :] = (section_in[tokens_of(m), :].astype(F32) + update).astype(BF)

    def sum_copy(k, device):
        return pltpu.make_async_remote_copy(
            src_ref=hsum.at[k],
            dst_ref=hgot.at[k],
            send_sem=sum_s.at[k],
            recv_sem=sum_r.at[k],
            device_id=device,
            device_id_type=MESH,
        )

    rounds = [y1, dp_peer, z1, z2, x1, x2]

    def sum_start(k):
        @pl.when(seg == 1)
        def _():
            sum_copy(k, rounds[k]).start()

    def sum_end(k):
        @pl.when(seg == 1)
        def _():
            sum_copy(k, rounds[k]).wait()
            hsum[k + 1] = hsum[k] + hgot[k]

    @pl.when(seg == 0)
    def _():
        to_next = seg_copy(out, inc, 0)
        to_next.start()
        to_next.wait_send()
        seg_copy(grad_ref, og_in, 1).wait_recv()
        og[...] = og_in[...]

    @pl.when(seg == 1)
    def _():
        hw = head_pad[...].astype(BF)
        o = out[...]
        logits = dot(hw, o, ((1,), (1,)))
        albedo = 1.0 / (1.0 + jnp.exp(-logits))
        row = lax.broadcasted_iota(jnp.int32, (8, TOKENS), 0)
        lane = lax.broadcasted_iota(jnp.int32, (8, TOKENS), 1)
        tint = jnp.zeros((8, TOKENS), F32)
        for m in range(MICROS):
            light = illum_ref[m, x]
            for c in range(3):
                tint = jnp.where((row == c) & (lane // HALF == m), light_ref[light, c], tint)
        mismatch = albedo * tint - targets[...]
        squares = jnp.sum(mismatch * mismatch)
        lg = (factor * mismatch * tint * albedo * (1.0 - albedo)).astype(BF)
        hg = dot(lg, o)
        row_h = lax.broadcasted_iota(jnp.int32, (8, CH), 0)
        hsum[0] = jnp.where(row_h == 3, squares, hg)
        lgt = lg.astype(F32).T.astype(BF)
        og[...] = dot(lgt, hw).astype(BF)

    sum_start(0)

    for m in range(MICROS):
        g = og[tokens_of(m), :].astype(F32)
        edges(2, m, g)
        fill(cat_c, m, g)
    halo_start(2)
    halo_wait(2, cat_c)
    sum_end(0)
    sum_start(1)
    for m in range(MICROS):
        sg = conv_back(cat_c, 1, m)
        hg = (sg * gelu_slope(hidden[tokens_of(m), :])).astype(BF).astype(F32)
        edges(3, m, hg)
        fill(cat_a, m, hg)
    halo_start(3)
    sum_end(1)
    sum_start(2)
    conv_weight_grad(x2t, cat_c, 1)
    halo_wait(3, cat_a)
    sum_end(2)
    sum_start(3)
    for m in range(MICROS):
        fg = conv_back(cat_a, 0, m)
        rows = tokens_of(m)
        slope = gelu_slope(section_in[rows, :].astype(F32))
        grad_ref[rows, :] = (og[rows, :].astype(F32) + fg * slope).astype(BF)

    @pl.when(seg == 1)
    def _():
        seg_copy(grad_ref, og_in, 1).start()

    sum_end(3)
    sum_start(4)
    conv_weight_grad(x1t, cat_a, 0)
    sum_end(4)
    sum_start(5)
    sum_end(5)

    final = pltpu.make_async_remote_copy(
        src_ref=hsum.at[6],
        dst_ref=hfin,
        send_sem=seg_s.at[2],
        recv_sem=seg_r.at[2],
        device_id=sibling,
        device_id_type=MESH,
    )

    @pl.when(seg == 1)
    def _():
        final.start()
        total_ref[...] = hsum[6]
        seg_copy(grad_ref, og_in, 1).wait_send()
        final.wait_send()

    @pl.when(seg == 0)
    def _():
        final.wait_recv()
        total_ref[...] = hfin[...]


class Reduce:
    def __init__(self, axis, own, store, stage, got, send, recv):
        self.a = axis
        self.own, self.store = own, store
        self.stage, self.got, self.send, self.recv = stage, got, send, recv
        self.copies = []

    def put(self, k, value, device):
        self.stage[k] = value.astype(BF)
        copy = pltpu.make_async_remote_copy(
            src_ref=self.stage.at[k],
            dst_ref=self.got.at[k],
            send_sem=self.send.at[k],
            recv_sem=self.recv.at[k],
            device_id=device,
            device_id_type=MESH,
        )
        copy.start()
        self.copies.append(copy)

    def take(self, k):
        pltpu.make_async_remote_copy(
            src_ref=self.stage.at[k],
            dst_ref=self.got.at[k],
            send_sem=self.send.at[k],
            recv_sem=self.recv.at[k],
            device_id=self.a.device(0, 1, 0),
            device_id_type=MESH,
        ).wait_recv()
        return self.got[k].astype(F32)

    def part(self, dp, r, dq):
        return self.own(self.a.slot(dp, r, dq))

    def first(self, i):
        dp, r = BACK[i]
        way = -1 if r == 0 else 1
        self.put(i, self.part(dp, r, 2), self.a.device(0, 0, way))
        self.put(16 + i, self.part(dp, r, -way), self.a.device(0, 0, -way))

    def second(self, i):
        dp, r = BACK[i]
        way = -1 if r == 0 else 1
        self.put(8 + i, self.part(dp, r, way) + self.take(i), self.a.device(0, 0, way))

    def third(self, i):
        dp, r = BACK[i]
        way = -1 if r == 0 else 1
        total = self.part(dp, r, 0) + self.take(8 + i) + self.take(16 + i)
        if dp == 2:
            self.put(24 + r, total, self.a.device(way, 0, 0))
        elif dp == way:
            self.put(26 + r, total + self.take(24 + r), self.a.device(way, 0, 0))
        elif dp == -way:
            self.put(28 + r, total, self.a.device(-way, 0, 0))
        else:
            total = total + self.take(26 + r) + self.take(28 + r)
            if r == 1:
                self.put(30, total, self.a.device(0, 1, 0))
            else:
                self.kept = total

    def fourth(self):
        self.kept = self.kept + self.take(30)
        self.put(31, self.kept, {"dp": 1 - lax.axis_index("dp")})

    def fifth(self):
        self.store(self.stage[31].astype(F32) + self.take(31))
        for copy in self.copies:
            copy.wait_send()


def reduce_kernel(
    hooks_ref,
    grad_ref,
    gconv_ref,
    proj_out,
    conv_out,
    hooks_v,
    part,
    pstage,
    pgot,
    cstage,
    cgot,
    load_sem,
    ps,
    pr,
    cs,
    cr,
):
    x, y, z = place()
    pa = Axis(True)
    loads = []
    for i, (dp, r) in enumerate(BACK):
        xs, ys, _ = pa.coords(dp, r, 0)
        start = pl.multiple_of((xs * 2 + ys) * CHUNK, CHUNK)
        copy = pltpu.make_async_copy(
            hooks_ref.at[:, pl.ds(start, CHUNK)], hooks_v.at[i], load_sem.at[i]
        )
        copy.start()
        loads.append(copy)
    entry_barrier(
        [
            at((x + 1) % 4, y, z),
            at((x + 3) % 4, y, z),
            at(x, y, (z + 1) % 4),
            at(x, y, (z + 3) % 4),
            at(x, 1 - y, z),
            {"dp": 1 - lax.axis_index("dp")},
        ]
    )

    def own_conv(slot):
        start = pl.multiple_of(slot * CSLOT, 8)
        return gconv_ref[:, pl.ds(start, CSLOT), :]

    def own_proj(slot):
        return part[slot]

    def store_conv(v):
        conv_out[...] = v

    def store_proj(v):
        proj_out[...] = v

    rc = Reduce(Axis(False), own_conv, store_conv, cstage, cgot, cs, cr)
    rp = Reduce(pa, own_proj, store_proj, pstage, pgot, ps, pr)

    def compute(i):
        loads[i].wait()
        dp, r = BACK[i]
        xs, ys, _ = pa.coords(dp, r, 0)
        base = xs * 8 + ys * 4
        v = dot(hooks_v[i], grad_ref[...], ((0,), (0,)))
        for k in range(4):
            part[base + k] = v[k * SLOT : (k + 1) * SLOT]

    rc.first(0)
    rc.first(1)
    for i in range(8):
        compute(i)
        rp.first(i)
        if i + 2 < 8:
            rc.first(i + 2)
        if i >= 1:
            rc.second(i - 1)
        if i >= 2:
            rp.second(i - 2)
    rc.second(7)
    rp.second(6)
    rp.second(7)
    for i in range(8):
        rc.third(i)
        rp.third(i)
    rc.fourth()
    rp.fourth()
    rc.fifth()
    rp.fifth()


def run_main(npix, factor, hooks, proj, conv, head, light, illum, offsets, photos):
    vm = pl.BlockSpec(memory_space=pltpu.VMEM)
    sm = pl.BlockSpec(memory_space=pltpu.SMEM)
    dma = pltpu.SemaphoreType.DMA
    return pl.pallas_call(
        functools.partial(main_kernel, npix, factor),
        out_shape=(
            jax.ShapeDtypeStruct((TOKENS, CH), BF),
            jax.ShapeDtypeStruct((2, 9 * CH, CH), F32),
            jax.ShapeDtypeStruct((8, CH), F32),
        ),
        in_specs=[pl.BlockSpec(memory_space=pl.ANY), vm, vm, vm, sm, sm, sm, vm],
        out_specs=(vm, vm, vm),
        scratch_shapes=[
            pltpu.VMEM((8, TOKENS, CHUNK), BF),
            pltpu.VMEM((32, SLOT, CH), BF),
            pltpu.VMEM((32, 2, CSLOT, CH), BF),
            pltpu.VMEM((2, 9 * CH, CH), F32),
            pltpu.VMEM((2, 9 * CH, CH), BF),
            pltpu.VMEM((TOKENS, CH), F32),
            pltpu.VMEM((TOKENS, CH), BF),
            pltpu.VMEM((TOKENS, CH), BF),
            pltpu.VMEM((TOKENS, CH), BF),
            pltpu.VMEM((TOKENS, CH), BF),
            pltpu.VMEM((TOKENS, CH), BF),
            pltpu.VMEM((TOKENS, CH), F32),
            pltpu.VMEM((MICROS, ROWS + 2, COLS, 3 * CH), BF),
            pltpu.VMEM((MICROS, ROWS + 2, COLS, 3 * CH), BF),
            pltpu.VMEM((MICROS, ROWS + 2, COLS, 3 * CH), BF),
            pltpu.VMEM((CH, TOKENS), BF),
            pltpu.VMEM((CH, TOKENS), BF),
            pltpu.VMEM((4, 2, MICROS, COLS, CH), BF),
            pltpu.VMEM((4, 2, MICROS, COLS, CH), BF),
            pltpu.VMEM((8, TOKENS), F32),
            pltpu.VMEM((8, CH), F32),
            pltpu.VMEM((7, 8, CH), F32),
            pltpu.VMEM((6, 8, CH), F32),
            pltpu.VMEM((8, CH), F32),
            dma((8,)),
            dma((32,)),
            dma((32,)),
            dma((32,)),
            dma((32,)),
            dma((4, 2)),
            dma((4, 2)),
            dma((3,)),
            dma((3,)),
            dma((6,)),
            dma((6,)),
        ],
        compiler_params=pltpu.CompilerParams(
            collective_id=0, has_side_effects=True, vmem_limit_bytes=56 * 1024 * 1024
        ),
        cost_estimate=pl.CostEstimate(
            flops=11_000_000_000, bytes_accessed=20_000_000, transcendentals=1_000_000
        ),
        name="main_kernel",
    )(hooks, proj, conv, head, light, illum, offsets, photos)


def run_reduce(hooks, grad, gconv):
    vm = pl.BlockSpec(memory_space=pltpu.VMEM)
    dma = pltpu.SemaphoreType.DMA
    return pl.pallas_call(
        reduce_kernel,
        out_shape=(
            jax.ShapeDtypeStruct((SLOT, CH), F32),
            jax.ShapeDtypeStruct((2, CSLOT, CH), F32),
        ),
        in_specs=[pl.BlockSpec(memory_space=pl.ANY), vm, vm],
        out_specs=(vm, vm),
        scratch_shapes=[
            pltpu.VMEM((8, TOKENS, CHUNK), BF),
            pltpu.VMEM((32, SLOT, CH), F32),
            pltpu.VMEM((32, SLOT, CH), BF),
            pltpu.VMEM((32, SLOT, CH), BF),
            pltpu.VMEM((32, 2, CSLOT, CH), BF),
            pltpu.VMEM((32, 2, CSLOT, CH), BF),
            dma((8,)),
            dma((32,)),
            dma((32,)),
            dma((32,)),
            dma((32,)),
        ],
        compiler_params=pltpu.CompilerParams(
            collective_id=1, has_side_effects=True, vmem_limit_bytes=56 * 1024 * 1024
        ),
        cost_estimate=pl.CostEstimate(
            flops=3_300_000_000, bytes_accessed=20_000_000, transcendentals=0
        ),
        name="reduce_kernel",
    )(hooks, grad, gconv)


def body(hooks, proj_weight, conv_weight, head_weight, light_color, illum, offsets, photos):
    npix = 3 * MICROS * lax.axis_size("dp") * ROWS * lax.axis_size("fsdp") * COLS
    factor = 2.0 * LOSS_SCALE / npix
    tokens = hooks.reshape(TOKENS, D)
    grad, gconv, total = run_main(
        npix, factor, tokens, proj_weight[0], conv_weight[0], head_weight, light_color,
        illum, offsets, photos,
    )
    grad_proj, grad_conv = run_reduce(tokens, grad, gconv)
    return (grad_proj[None], grad_conv[None], total[:3], total[3, 0] / npix)


def solution(mesh):
    placed = (
        P("segment", "dp", "fsdp", None, None),
        P("segment", "fsdp", None),
        P("segment", None, "fsdp", None),
        P(),
        P(),
        P("dp", None),
        P("dp", None, None),
        P("dp", None, None, None, None),
    )
    return jax.shard_map(
        body,
        mesh=mesh,
        in_specs=placed,
        out_specs=(P("segment", "fsdp", None), P("segment", None, "fsdp", None), P(), P()),
        check_vma=False,
    )
```

time: 890 us -> 163 us (0.18)
  waiting for transfers between devices: 636 us -> 0 us
  Pallas kernels: 0 us -> 153 us
  blocking collectives: 65.7 us -> 0 us
  local copies, waits for them, and re-layouts: 62.2 us -> 7.04 us
  starting transfers between devices: 45.5 us -> 0 us
  matrix products: 41.6 us -> 0 us
  between operations: 17.8 us -> 2.45 us
  other arithmetic: 12.8 us -> 0 us
    unnamed x7 -> x0, waiting for transfers between devices: 313 us -> none
    all_gather x2 -> x0, waiting for transfers between devices: 289 us -> none  [the longest x1 158 us: body(): lax.all_gather(proj_weight[0], 'fsdp', axis=0, tiled=True)]
    pallas_call x0 -> x2, Pallas kernels: none -> 153 us  [the longest x1 108 us: run_main(): pl.pallas_call(functools.partial(main_kernel, npix, factor), out_shape=(j...]
    psum x1 -> x0, blocking collectives: 65.7 us -> none  [body(): lax.psum((head_term, loss_term), ('segment', 'fsdp', 'dp'))]
    ppermute x18 -> x0, starting transfers between devices: 45.3 us -> none  [the longest x8 31.5 us: extended(): before = lax.ppermute(last, axis, up)]
    dot_general x15 -> x0, matrix products: 41.6 us -> none  [the longest x3 18.9 us: contract_rows(): lax.dot_general(left, right, (((0,), (0,)), ((), ())), preferred_element_...]
    unnamed x114 -> x6, local copies, waits for them, and re-layouts: 46.8 us -> 5.93 us
    ppermute x18 -> x0, waiting for transfers between devices: 34.7 us -> none  [the longest x8 27.7 us: extended(): after = lax.ppermute(initial, axis, down)]
  transfers between devices with their start and end apart: 23 -> 0, of which waited for: 17 -> 0; matrix products, arithmetic and copies ran while one was open for 8% -> 0% of each run, Pallas kernels for 0% -> 0%
where the time goes in v1:
time: 163 us
  Pallas kernels  153 us (94%)
  local copies, waits for them, and re-layouts  7.04 us (4%)
  between operations  2.45 us (2%)
    pallas_call x1, Pallas kernels, run_main(): pl.pallas_call(functools.partial(main_kernel, npix, factor), out_shape=(j...  108 us
    pallas_call x1, Pallas kernels, run_reduce(): pl.pallas_call(reduce_kernel, out_shape=(jax.ShapeDtypeStruct((SLOT, CH),...  45.7 us
    unnamed x6, local copies, waits for them, and re-layouts  5.93 us

profile of v1, /device:TPU:0, one launch (start us, length us, event | category | flops | bytes accessed | tf_op | source)
XLA Modules:
  0.0 162.8 jit_solution(14814600077400357965)
XLA Ops:
  0.6 1.4 copy.12.light_ref
  2.0 1.4 copy.13.offsets_ref
  3.4 107.6 %main_kernel.1 = (bf16[1024,256]{1,0:T(8,128)(2,1)}, f32[2,2304,256]{2,1,0:T(8,128)}, f32[8,256]{1,0:T(8,128)}) custom-call(bf16[1024,6144]{1,0:T(8,128)(2,1)} %bitcast.6, bf16[192,256]{1,0:T(8,128)(2,1)} %bitcast.10, bf16[2,72,256]{2,1,0:T(8,128)(2,1)} %bitcast.11, bf16[3,256]{1,0:T(4,128)(2,1)} %head_ref.1, f32[25,3]{1,0:T(8,128)} %copy.12.light_ref, ...), custom_call_target="tpu_custom_call" | custom-call | flops 11000000512 | bytes 20000000 | tf_op jit(solution)/shard_map/main_kernel/pallas_call | solution.py:727
  110.9 0.0 copy-start
  111.0 45.7 %reduce_kernel.1 = (f32[192,256]{1,0:T(8,128)}, f32[2,72,256]{2,1,0:T(8,128)}) custom-call(bf16[1024,6144]{1,0:T(8,128)(2,1)} %bitcast.7, bf16[1024,256]{1,0:T(8,128)(2,1)} %get-tuple-element.9.grad_ref, f32[2,2304,256]{2,1,0:T(8,128)} %get-tuple-element.10.gconv_ref), custom_call_target="tpu_custom_call" | custom-call | flops 3300000000 | bytes 20000000 | tf_op jit(solution)/shard_map/reduce_kernel/pallas_call | solution.py:786
  156.7 0.0 copy-done
  156.7 0.6 slice.6
  157.3 0.5 slice.7
  158.4 1.6 copy.16
  160.0 1.6 copy.17
Async XLA Ops:
  110.9 45.7 %copy-start = (f32[8,256]{1,0:T(8,128)S(1)}, f32[8,256]{1,0:T(8,128)}, u32[]{:S(2)}) copy-start(f32[8,256]{1,0:T(8,128)} %get-tuple-element.13) | copy-start | bytes 24580

commit v2 on v1

v2 whole, which is shorter than its diff:
```python
import functools

import jax
import jax.numpy as jnp
from jax import lax
from jax.experimental import pallas as pl
from jax.experimental.pallas import tpu as pltpu
from jax.sharding import PartitionSpec as P

LOSS_SCALE = 8192.0
MESH = pl.DeviceIdType.MESH
BF = jnp.bfloat16
F32 = jnp.float32

MICROS, ROWS, COLS, CH = 2, 8, 64, 256
TOKENS = MICROS * ROWS * COLS
HALF = ROWS * COLS
D = 6144
SLOT = 192
CSLOT = 72
CHUNK = 4 * SLOT

ORDER = [(0, 0), (1, 0), (-1, 0), (0, 1), (2, 0), (1, 1), (-1, 1), (2, 1)]
PLANE = ORDER[1:]
BACK = ORDER[::-1]


def place():
    f = lax.axis_index("fsdp")
    return f // 8, (f // 4) % 2, f % 4


def at(x, y, z):
    return {"fsdp": x * 8 + y * 4 + z}


def dot(a, b, dims=((1,), (0,))):
    return lax.dot_general(a, b, (dims, ((), ())), preferred_element_type=F32)


def gelu_parts(v):
    c = 0.7978845608028654
    t = jnp.tanh(c * (v + 0.044715 * (v * v * v)))
    return t


def gelu(v):
    return 0.5 * v * (1.0 + gelu_parts(v))


def gelu_slope(v):
    c = 0.7978845608028654
    t = gelu_parts(v)
    return 0.5 * (1.0 + t) + 0.5 * v * (1.0 - t * t) * (c * (1.0 + 3.0 * 0.044715 * (v * v)))


class Axis:
    def __init__(self, p_is_x):
        x, y, z = place()
        self.p_is_x = p_is_x
        self.p, self.y, self.q = (x, y, z) if p_is_x else (z, y, x)

    def coords(self, dp, r, dq):
        p = (self.p + (dp + 4)) % 4
        q = (self.q + (dq + 4)) % 4
        y = (self.y + r) % 2
        return (p, y, q) if self.p_is_x else (q, y, p)

    def slot(self, dp, r, dq):
        x, y, z = self.coords(dp, r, dq)
        return x * 8 + y * 4 + z

    def device(self, dp, r, dq):
        return at(*self.coords(dp, r, dq))


def rel(dp, r, dq):
    return ((dp % 4) * 2 + r) * 4 + dq % 4


class Gather:
    def __init__(self, axis, buf, send, recv):
        self.a, self.buf, self.send, self.recv = axis, buf, send, recv
        self.copies = []

    def put(self, dp, r, dq, to):
        tp, tr, tq = to
        a = self.a
        slot = a.slot(dp, r, dq)
        copy = pltpu.make_async_remote_copy(
            src_ref=self.buf.at[slot],
            dst_ref=self.buf.at[slot],
            send_sem=self.send.at[len(self.copies)],
            recv_sem=self.recv.at[rel(dp - tp, (r + tr) % 2, dq - tq)],
            device_id=a.device(tp, tr, tq),
            device_id_type=MESH,
        )
        copy.start()
        self.copies.append(copy)

    def await_(self, dp, r, dq):
        a = self.a
        slot = a.slot(dp, r, dq)
        pltpu.make_async_remote_copy(
            src_ref=self.buf.at[slot],
            dst_ref=self.buf.at[slot],
            send_sem=self.send.at[0],
            recv_sem=self.recv.at[rel(dp, r, dq)],
            device_id=a.device(0, 1, 0),
            device_id_type=MESH,
        ).wait_recv()

    def spread(self):
        for dp, r in PLANE:
            self.put(0, 0, 0, (dp, r, 0))

    def along(self, i):
        dp, r = ORDER[i]
        if i > 0:
            self.await_(dp, r, 0)
        for dq in (1, -1, 2):
            self.put(dp, r, 0, (0, 0, dq))

    def last(self, i):
        dp, r = ORDER[i]
        for dq in (1, -1, 2):
            self.await_(dp, r, dq)

    def drain(self):
        for copy in self.copies:
            copy.wait_send()


def entry_barrier(devices):
    barrier = pltpu.get_barrier_semaphore()
    for device in devices:
        pl.semaphore_signal(barrier, inc=1, device_id=device, device_id_type=MESH)
    pl.semaphore_wait(barrier, len(devices))


def partners():
    pa, pc = Axis(True), Axis(False)
    return [pa.device(dp, r, 0) for dp, r in PLANE] + [
        pc.device(dp, r, 0) for dp, r in PLANE if dp != 0
    ]


def load_rows(source, target, sem):
    copies = []
    for i in range(8):
        rows = pl.ds(i * (TOKENS // 8), TOKENS // 8)
        copy = pltpu.make_async_copy(source.at[rows, :], target.at[rows, :], sem.at[i])
        copy.start()
        copies.append(copy)
    return copies


def shift_parts(v):
    n = v.shape[0]
    col = lax.broadcasted_iota(jnp.int32, v.shape, 0) % COLS
    before = jnp.where(col == 0, 0.0, pltpu.roll(v, 1, 0))
    after = jnp.where(col == COLS - 1, 0.0, pltpu.roll(v, n - 1, 0))
    return before.astype(BF), v.astype(BF), after.astype(BF)


class Reduce:
    def __init__(self, axis, own, store, stage, got, send, recv, placed=False):
        self.a = axis
        self.own, self.store = own, store
        self.stage, self.got, self.send, self.recv = stage, got, send, recv
        self.placed = placed
        self.copies = []

    def put(self, k, value, device):
        if value is not None:
            self.stage[k] = value.astype(BF)
        copy = pltpu.make_async_remote_copy(
            src_ref=self.stage.at[k],
            dst_ref=self.got.at[k],
            send_sem=self.send.at[k],
            recv_sem=self.recv.at[k],
            device_id=device,
            device_id_type=MESH,
        )
        copy.start()
        self.copies.append(copy)

    def take(self, k):
        pltpu.make_async_remote_copy(
            src_ref=self.stage.at[k],
            dst_ref=self.got.at[k],
            send_sem=self.send.at[k],
            recv_sem=self.recv.at[k],
            device_id=self.a.device(0, 1, 0),
            device_id_type=MESH,
        ).wait_recv()
        return self.got[k].astype(F32)

    def part(self, dp, r, dq, i):
        return self.own(self.a.slot(dp, r, dq), dq, i)

    def first(self, i):
        dp, r = BACK[i]
        for j, dq in enumerate((2, 1, -1)):
            value = None if self.placed else self.part(dp, r, dq, i)
            self.put(3 * i + j, value, self.a.device(0, 0, dq))

    def second(self, i):
        dp, r = BACK[i]
        total = self.part(dp, r, 0, i)
        for j in range(3):
            total = total + self.take(3 * i + j)
        if i < 7:
            self.put(24 + i, total, self.a.device(dp, r, 0))
        else:
            self.kept = total

    def third(self):
        for i in range(7):
            self.kept = self.kept + self.take(24 + i)
        self.put(31, self.kept, {"dp": 1 - lax.axis_index("dp")})

    def fourth(self):
        self.store(self.stage[31].astype(F32) + self.take(31))
        for copy in self.copies:
            copy.wait_send()


def main_kernel(
    factor,
    hooks_ref,
    proj_ref,
    conv_ref,
    head_ref,
    light_ref,
    illum_ref,
    offsets_ref,
    photos_ref,
    proj_out,
    conv_out,
    total_ref,
    hooks_v,
    wproj,
    wconv,
    wf32,
    wbf,
    wflip,
    acc,
    section_in,
    inc,
    out,
    og_in,
    og,
    grad,
    hidden,
    cat_a,
    cat_b,
    cat_c,
    cat_d,
    x1t,
    x2t,
    hsend,
    hrecv,
    targets,
    head_pad,
    hsum,
    hgot,
    hfin,
    part,
    pgot,
    cgot,
    load_sem,
    psend,
    precv,
    csend,
    crecv,
    hs_sem,
    hr_sem,
    seg_s,
    seg_r,
    sum_s,
    sum_r,
    rps,
    rpr,
    rcs,
    rcr,
    gate,
):
    x, y, z = place()
    seg = lax.axis_index("segment")
    dpi = lax.axis_index("dp")
    band = y * 4 + z
    sibling = {"segment": 1 - seg}
    dp_peer = {"dp": 1 - dpi}
    up_j, down_j = (band + 7) % 8, (band + 1) % 8
    up = at(x, up_j // 4, up_j % 4)
    down = at(x, down_j // 4, down_j % 4)
    up_other = {"segment": 1 - seg, **up}
    down_other = {"segment": 1 - seg, **down}

    pa = Axis(True)
    loads = load_rows(hooks_ref, hooks_v, load_sem)

    me = x * 8 + y * 4 + z
    wproj[me] = proj_ref[...]
    wconv[me] = conv_ref[...]

    z1 = at(x, y, z + 1 - 2 * (z % 2))
    z2 = at(x, y, (z + 2) % 4)
    x1 = at(x + 1 - 2 * (x % 2), y, z)
    x2 = at((x + 2) % 4, y, z)
    y1 = at(x, 1 - y, z)
    entry_barrier(partners() + [sibling, dp_peer, up_other, down_other])

    gp = Gather(pa, wproj, psend, precv)
    gc = Gather(Axis(False), wconv, csend, crecv)

    @pl.when(seg == 1)
    def _():
        pl.semaphore_wait(gate, 1)

    gp.spread()
    gc.spread()
    gp.along(0)
    gc.along(0)

    yy = lax.broadcasted_iota(jnp.int32, (96, HALF), 0)
    nn = lax.broadcasted_iota(jnp.int32, (96, HALF), 1)
    row8 = lax.broadcasted_iota(jnp.int32, (8, HALF), 0)
    for m in range(MICROS):
        oy = offsets_ref[m, 0, x]
        ox = offsets_ref[m, 1, x]
        pick_col = (yy == ox + nn % COLS).astype(F32).astype(BF)
        pick_row = yy == oy + band * ROWS + nn // COLS
        block = jnp.zeros((8, HALF), F32)
        for c in range(3):
            q = dot(photos_ref[m, x, c], pick_col)
            line = jnp.sum(jnp.where(pick_row, q, 0.0), axis=0, keepdims=True)
            block = jnp.where(row8 == c, line, block)
        targets[:, m * HALF : (m + 1) * HALF] = block
    head_pad[...] = jnp.zeros((8, CH), F32)
    head_pad[0:3, :] = head_ref[...].astype(F32)

    acc[...] = jnp.zeros_like(acc)
    for copy in loads:
        copy.wait()

    def project(i):
        dp, r = ORDER[i]
        xs, ys, _ = pa.coords(dp, r, 0)
        base = xs * 8 + ys * 4
        lanes = pl.ds(pl.multiple_of(base * SLOT, CHUNK), CHUNK)
        w = wproj[pl.ds(base, 4)].reshape(CHUNK, CH)

        def step(t, _):
            rows = pl.ds(pl.multiple_of(t * 256, 256), 256)
            acc[rows, :] += dot(hooks_v[rows, lanes], w)
            return 0

        lax.fori_loop(0, TOKENS // 256, step, 0)

    for i in range(1, 8):
        gp.along(i)
        gc.along(i)
        if i == 7:

            @pl.when(seg == 0)
            def _():
                pl.semaphore_signal(gate, inc=1, device_id=sibling, device_id_type=MESH)

        if i >= 2:
            gp.last(i - 2)
            gc.last(i - 2)
            project(i - 2)
    gc.last(6)
    gc.last(7)

    def gather_rows(k, _):
        start = pl.multiple_of(k * CSLOT, 8)
        wf32[0, pl.ds(start, CSLOT), :] = wconv[k, 0].astype(F32)
        wf32[1, pl.ds(start, CSLOT), :] = wconv[k, 1].astype(F32)
        return 0

    lax.fori_loop(0, 32, gather_rows, 0)

    def to_bf(k, _):
        start = pl.multiple_of(k * CH, CH)
        wbf[0, pl.ds(start, CH), :] = wf32[0, pl.ds(start, CH), :].astype(BF)
        wbf[1, pl.ds(start, CH), :] = wf32[1, pl.ds(start, CH), :].astype(BF)
        return 0

    lax.fori_loop(0, 9, to_bf, 0)
    gp.last(6)
    project(6)
    gp.last(7)
    project(7)

    def flip_weights():
        def step(k, _):
            source = pl.ds(pl.multiple_of(k * CH, CH), CH)
            target = pl.ds(pl.multiple_of((8 - k) * CH, CH), CH)
            wflip[0, target, :] = wf32[0, source, :].T.astype(BF)
            wflip[1, target, :] = wf32[1, source, :].T.astype(BF)
            return 0

        lax.fori_loop(0, 9, step, 0)

    def seg_copy(src, dst, k):
        return pltpu.make_async_remote_copy(
            src_ref=src,
            dst_ref=dst,
            send_sem=seg_s.at[k],
            recv_sem=seg_r.at[k],
            device_id=sibling,
            device_id_type=MESH,
        )

    def halo(e, side, device):
        return pltpu.make_async_remote_copy(
            src_ref=hsend.at[e, side],
            dst_ref=hrecv.at[e, 1 - side],
            send_sem=hs_sem.at[e, side],
            recv_sem=hr_sem.at[e, 1 - side],
            device_id=device,
            device_id_type=MESH,
        )

    def halo_start(e, to_up, to_down):
        halo(e, 0, to_up).start()
        halo(e, 1, to_down).start()

    def halo_sent(e):
        halo(e, 0, up).wait_send()
        halo(e, 1, up).wait_send()

    def halo_here(e):
        halo(e, 0, up).wait_recv()
        halo(e, 1, up).wait_recv()

    def edges(e, source):
        for m in range(MICROS):
            hsend[e, 0, m] = source[m * HALF : m * HALF + 2 * COLS, :]
            hsend[e, 1, m] = source[(m + 1) * HALF - 2 * COLS : (m + 1) * HALF, :]

    def fill(cat, m, row, value):
        a, b, c = shift_parts(value)
        n = value.shape[0] // COLS
        cat[m, row : row + n, :, 0:CH] = a.reshape(n, COLS, CH)
        cat[m, row : row + n, :, CH : 2 * CH] = b.reshape(n, COLS, CH)
        cat[m, row : row + n, :, 2 * CH : 3 * CH] = c.reshape(n, COLS, CH)

    def tokens_of(m):
        return slice(m * HALF, (m + 1) * HALF)

    def conv(weights, which, left):
        total = None
        for ky in range(3):
            value = left(ky)
            value = value.reshape(-1, 3 * CH)
            piece = dot(value, weights[which, ky * 3 * CH : (ky + 1) * 3 * CH, :])
            total = piece if total is None else total + piece
        return total

    def conv_weight_grad(xt, cat, low, which):
        for ky in range(3):
            total = None
            for m in range(MICROS):
                right = cat[m, low - ky : low - ky + ROWS].reshape(HALF, 3 * CH)
                piece = dot(xt[:, tokens_of(m)], right)
                total = piece if total is None else total + piece
            for kx in range(3):
                j = 2 - kx
                row = (3 * ky + kx) * CH
                wf32[which, row : row + CH, :] = total[:, j * CH : (j + 1) * CH]

    def two_convs(cat, weights, first, middle, mid, second, halo_ready):
        for m in range(MICROS):
            v = conv(weights, first, lambda ky: cat[m, 2 + ky : 8 + ky])
            fill(mid, m, 2, middle(m, 1, 6, v))
        halo_ready()
        for low, edge in ((0, 0), (8, 7)):
            v = conv(weights, first, lambda ky: cat[:, low + ky : low + ky + 2])
            for m in range(MICROS):
                u = middle(m, low - 1, 2, v[m * 2 * COLS : (m + 1) * 2 * COLS])
                outer = lax.broadcasted_iota(jnp.int32, u.shape, 0) // COLS == edge // 7
                u = jnp.where(jnp.logical_and(outer, band == edge), 0.0, u)
                fill(mid, m, low, u)
        return [conv(weights, second, lambda ky, m=m: mid[m, ky : ky + ROWS]) for m in range(MICROS)]

    def halo_rows(cat, rows_of):
        for side, row, last in ((0, 0, 0), (1, ROWS + 2, 7)):
            for m in range(MICROS):
                v = rows_of(side, m)
                v = jnp.where(band == last, jnp.zeros_like(v), v)
                fill(cat, m, row, v)

    section_in[...] = acc[...].astype(BF)
    edges(0, section_in)
    halo_start(0, up, down)
    gp.drain()
    gc.drain()

    @pl.when(seg == 1)
    def _():
        flip_weights()
        seg_copy(out, inc, 0).wait_recv()
        section_in[...] = (section_in[...].astype(F32) + inc[...].astype(F32)).astype(BF)

    for m in range(MICROS):
        fill(cat_a, m, 2, gelu(section_in[tokens_of(m), :].astype(F32)).astype(BF).astype(F32))

    def forward_halo():
        halo_here(0)

        @pl.when(seg == 1)
        def _():
            halo_here(1)

        def rows_of(side, m):
            shape = (2 * COLS, CH)
            more = jnp.where(seg == 1, hrecv[1, side, m].astype(F32), 0.0)
            v = (hrecv[0, side, m].astype(F32) + more).astype(BF).astype(F32)
            return gelu(v).astype(BF).astype(F32)

        halo_rows(cat_a, rows_of)

    def keep_hidden(m, row, n, v):
        hidden[m, row + 1 : row + 1 + n] = v.reshape(n, COLS, CH)
        return gelu(v).astype(BF).astype(F32)

    update = two_convs(cat_a, wbf, 0, keep_hidden, cat_b, 1, forward_halo)
    for m in range(MICROS):
        out[tokens_of(m), :] = (section_in[tokens_of(m), :].astype(F32) + update[m]).astype(BF)

    def transposes():
        for m in range(MICROS):
            v = cat_a[m, 2 : 2 + ROWS, :, CH : 2 * CH].reshape(HALF, CH).astype(F32)
            x1t[:, tokens_of(m)] = v.T.astype(BF)
            v = cat_b[m, 1 : 1 + ROWS, :, CH : 2 * CH].reshape(HALF, CH).astype(F32)
            x2t[:, tokens_of(m)] = v.T.astype(BF)

    def sum_copy(k, device):
        return pltpu.make_async_remote_copy(
            src_ref=hsum.at[k],
            dst_ref=hgot.at[k],
            send_sem=sum_s.at[k],
            recv_sem=sum_r.at[k],
            device_id=device,
            device_id_type=MESH,
        )

    rounds = [y1, dp_peer, z1, z2, x1, x2]

    def sum_start(k):
        @pl.when(seg == 1)
        def _():
            sum_copy(k, rounds[k]).start()

    def sum_end(k):
        @pl.when(seg == 1)
        def _():
            sum_copy(k, rounds[k]).wait()
            hsum[k + 1] = hsum[k] + hgot[k]

    @pl.when(seg == 0)
    def _():
        edges(1, out)
        halo_start(1, up_other, down_other)
        to_next = seg_copy(out, inc, 0)
        to_next.start()
        flip_weights()
        transposes()
        to_next.wait_send()
        halo_sent(1)
        seg_copy(grad, og_in, 1).wait_recv()
        og[...] = og_in[...]

    @pl.when(seg == 1)
    def _():
        hw = head_pad[...].astype(BF)
        o = out[...]
        logits = dot(hw, o, ((1,), (1,)))
        albedo = 1.0 / (1.0 + jnp.exp(-logits))
        row = lax.broadcasted_iota(jnp.int32, (8, TOKENS), 0)
        lane = lax.broadcasted_iota(jnp.int32, (8, TOKENS), 1)
        tint = jnp.zeros((8, TOKENS), F32)
        for m in range(MICROS):
            light = illum_ref[m, x]
            for c in range(3):
                tint = jnp.where((row == c) & (lane // HALF == m), light_ref[c, light], tint)
        mismatch = albedo * tint - targets[...]
        lg = (factor * mismatch * tint * albedo * (1.0 - albedo)).astype(BF)
        lgt = lg.astype(F32).T.astype(BF)
        og[...] = dot(lgt, hw).astype(BF)
        edges(2, og)
        halo_start(2, up, down)
        squares = jnp.sum(mismatch * mismatch)
        hg = dot(lg, o)
        row_h = lax.broadcasted_iota(jnp.int32, (8, CH), 0)
        hsum[0] = jnp.where(row_h == 3, squares, hg)

    sum_start(0)

    for m in range(MICROS):
        fill(cat_c, m, 2, og[tokens_of(m), :].astype(F32))

    def backward_halo():
        @pl.when(seg == 1)
        def _():
            halo_here(2)

        @pl.when(seg == 0)
        def _():
            halo_here(3)

        def rows_of(side, m):
            v = jnp.where(seg == 1, hrecv[2, side, m].astype(F32), hrecv[3, side, m].astype(F32))
            return v

        halo_rows(cat_c, rows_of)

    def through(m, row, n, v):
        h = hidden[m, row + 1 : row + 1 + n].reshape(n * COLS, CH)
        return (v * gelu_slope(h)).astype(BF).astype(F32)

    back = two_convs(cat_c, wflip, 1, through, cat_d, 0, backward_halo)
    for m in range(MICROS):
        rows = tokens_of(m)
        slope = gelu_slope(section_in[rows, :].astype(F32))
        grad[rows, :] = (og[rows, :].astype(F32) + back[m] * slope).astype(BF)

    @pl.when(seg == 1)
    def _():
        edges(3, grad)
        halo_start(3, up_other, down_other)
        seg_copy(grad, og_in, 1).start()
        transposes()

    sum_end(0)
    sum_start(1)
    conv_weight_grad(x2t, cat_c, 3, 1)
    sum_end(1)
    sum_start(2)
    conv_weight_grad(x1t, cat_d, 2, 0)
    sum_end(2)
    sum_start(3)

    def own_conv(slot, dq, i):
        start = pl.multiple_of(slot * CSLOT, 8)
        return wf32[:, pl.ds(start, CSLOT), :]

    def own_proj(slot, dq, i):
        return part[i]

    def store_conv(v):
        conv_out[...] = v

    def store_proj(v):
        proj_out[...] = v

    rc = Reduce(Axis(False), own_conv, store_conv, wconv, cgot, rcs, rcr)
    rp = Reduce(pa, own_proj, store_proj, wproj, pgot, rps, rpr, placed=True)

    def compute(i):
        dp, r = BACK[i]
        xs, ys, _ = pa.coords(dp, r, 0)
        base = xs * 8 + ys * 4
        lanes = pl.ds(pl.multiple_of(base * SLOT, CHUNK), CHUNK)
        v = dot(hooks_v[:, lanes], grad[...], ((0,), (0,)))
        for k in range(4):
            ahead = (k - z + 4) % 4
            block = v[k * SLOT : (k + 1) * SLOT]
            for dq, j in ((0, None), (2, 0), (1, 1), (3, 2)):

                @pl.when(ahead == dq)
                def _():
                    if j is None:
                        part[i] = block
                    else:
                        wproj[3 * i + j] = block.astype(BF)

        rp.first(i)

    for i in range(8):
        rc.first(i)
        compute(i)
        if i in (1, 3, 5):
            sum_end(3 + i // 2)
            if i < 5:
                sum_start(4 + i // 2)
        if i >= 2:
            rc.second(i - 2)
            rp.second(i - 2)
    final = pltpu.make_async_remote_copy(
        src_ref=hsum.at[6],
        dst_ref=hfin,
        send_sem=seg_s.at[2],
        recv_sem=seg_r.at[2],
        device_id=sibling,
        device_id_type=MESH,
    )

    @pl.when(seg == 1)
    def _():
        final.start()
        total_ref[...] = hsum[6]

    for i in (6, 7):
        rc.second(i)
        rp.second(i)
    rc.third()
    rp.third()
    rc.fourth()
    rp.fourth()
    halo_sent(0)

    @pl.when(seg == 1)
    def _():
        halo_sent(2)
        halo_sent(3)
        seg_copy(grad, og_in, 1).wait_send()
        final.wait_send()

    @pl.when(seg == 0)
    def _():
        final.wait_recv()
        total_ref[...] = hfin[...]


def run_main(factor, hooks, proj, conv, head, light, illum, offsets, photos):
    vm = pl.BlockSpec(memory_space=pltpu.VMEM)
    sm = pl.BlockSpec(memory_space=pltpu.SMEM)
    dma = pltpu.SemaphoreType.DMA
    field = pltpu.VMEM((TOKENS, CH), BF)
    return pl.pallas_call(
        functools.partial(main_kernel, factor),
        out_shape=(
            jax.ShapeDtypeStruct((SLOT, CH), F32),
            jax.ShapeDtypeStruct((2, CSLOT, CH), F32),
            jax.ShapeDtypeStruct((8, CH), F32),
        ),
        in_specs=[pl.BlockSpec(memory_space=pl.ANY), vm, vm, vm, sm, sm, sm, vm],
        out_specs=(vm, vm, vm),
        scratch_shapes=[
            pltpu.VMEM((TOKENS, D), BF),
            pltpu.VMEM((32, SLOT, CH), BF),
            pltpu.VMEM((32, 2, CSLOT, CH), BF),
            pltpu.VMEM((2, 9 * CH, CH), F32),
            pltpu.VMEM((2, 9 * CH, CH), BF),
            pltpu.VMEM((2, 9 * CH, CH), BF),
            pltpu.VMEM((TOKENS, CH), F32),
            field,
            field,
            field,
            field,
            field,
            field,
            pltpu.VMEM((MICROS, ROWS + 2, COLS, CH), F32),
            pltpu.VMEM((MICROS, ROWS + 4, COLS, 3 * CH), BF),
            pltpu.VMEM((MICROS, ROWS + 2, COLS, 3 * CH), BF),
            pltpu.VMEM((MICROS, ROWS + 4, COLS, 3 * CH), BF),
            pltpu.VMEM((MICROS, ROWS + 2, COLS, 3 * CH), BF),
            pltpu.VMEM((CH, TOKENS), BF),
            pltpu.VMEM((CH, TOKENS), BF),
            pltpu.VMEM((4, 2, MICROS, 2 * COLS, CH), BF),
            pltpu.VMEM((4, 2, MICROS, 2 * COLS, CH), BF),
            pltpu.VMEM((8, TOKENS), F32),
            pltpu.VMEM((8, CH), F32),
            pltpu.VMEM((7, 8, CH), F32),
            pltpu.VMEM((6, 8, CH), F32),
            pltpu.VMEM((8, CH), F32),
            pltpu.VMEM((8, SLOT, CH), F32),
            pltpu.VMEM((32, SLOT, CH), BF),
            pltpu.VMEM((32, 2, CSLOT, CH), BF),
            dma((8,)),
            dma((32,)),
            dma((32,)),
            dma((32,)),
            dma((32,)),
            dma((4, 2)),
            dma((4, 2)),
            dma((3,)),
            dma((3,)),
            dma((6,)),
            dma((6,)),
            dma((32,)),
            dma((32,)),
            dma((32,)),
            dma((32,)),
            pltpu.SemaphoreType.REGULAR,
        ],
        compiler_params=pltpu.CompilerParams(
            collective_id=0, has_side_effects=True, vmem_limit_bytes=60 * 1024 * 1024
        ),
        cost_estimate=pl.CostEstimate(
            flops=15_000_000_000, bytes_accessed=14_000_000, transcendentals=1_000_000
        ),
        name="main_kernel",
    )(hooks, proj, conv, head, light, illum, offsets, photos)


def body(hooks, proj_weight, conv_weight, head_weight, light_color, illum, offsets, photos):
    npix = 3 * MICROS * lax.axis_size("dp") * ROWS * lax.axis_size("fsdp") * COLS
    factor = 2.0 * LOSS_SCALE / npix
    tokens = hooks.reshape(TOKENS, D)
    grad_proj, grad_conv, total = run_main(
        factor, tokens, proj_weight[0], conv_weight[0], head_weight, light_color.T,
        illum, offsets.transpose(0, 2, 1), photos,
    )
    return (grad_proj[None], grad_conv[None], total[:3], total[3, 0] / npix)


def solution(mesh):
    placed = (
        P("segment", "dp", "fsdp", None, None),
        P("segment", "fsdp", None),
        P("segment", None, "fsdp", None),
        P(),
        P(),
        P("dp", None),
        P("dp", None, None),
        P("dp", None, None, None, None),
    )
    return jax.shard_map(
        body,
        mesh=mesh,
        in_specs=placed,
        out_specs=(P("segment", "fsdp", None), P("segment", None, "fsdp", None), P(), P()),
        check_vma=False,
    )
```

time: 163 us -> 138 us (0.85)
  Pallas kernels: 153 us -> 130 us
    pallas_call x2 -> x1, Pallas kernels: 153 us -> 130 us  [run_main(): pl.pallas_call(functools.partial(main_kernel, factor), out_shape=(jax.Sha...]
    unnamed x6 -> x2, local copies, waits for them, and re-layouts: 5.93 us -> 3.2 us
where the time goes in v2:
time: 138 us
  Pallas kernels  130 us (94%)
  local copies, waits for them, and re-layouts  5.67 us (4%)
  between operations  2.43 us (2%)
    pallas_call x1, Pallas kernels, run_main(): pl.pallas_call(functools.partial(main_kernel, factor), out_shape=(jax.Sha...  130 us
    unnamed x2, local copies, waits for them, and re-layouts  3.2 us

profile of v2, /device:TPU:0, one launch (start us, length us, event | category | flops | bytes accessed | tf_op | source)
XLA Modules:
  0.0 138.2 jit_solution(10700980269299959929)
XLA Ops:
  0.6 130.1 %main_kernel.1 = (f32[192,256]{1,0:T(8,128)}, f32[2,72,256]{2,1,0:T(8,128)}, f32[8,256]{1,0:T(8,128)}) custom-call(bf16[1024,6144]{1,0:T(8,128)(2,1)} %bitcast.10, bf16[192,256]{1,0:T(8,128)(2,1)} %bitcast.11, bf16[2,72,256]{2,1,0:T(8,128)(2,1)} %bitcast.12, bf16[3,256]{1,0:T(4,128)(2,1)} %head_ref.1, f32[3,25]{1,0:T(4,128)} %bitcast.13, s32[2,4]{1,0:T(2,128)} %illum_ref.1, ...), custom_call_target="tpu_custom_call" | custom-call | flops 15000000512 | bytes 14000000 | tf_op jit(solution)/shard_map/main_kernel/pallas_call | solution.py:735
  130.7 1.3 slice.6
  132.0 1.2 slice.7
  133.9 1.6 %copy.14 = f32[1,192,256]{2,1,0:T(8,128)} copy(f32[1,192,256]{2,1,0:T(8,128)} %bitcast.8) | data formatting | bytes 393216
  135.5 1.6 %copy.15 = f32[1,2,72,256]{3,2,1,0:T(8,128)} copy(f32[1,2,72,256]{3,2,1,0:T(8,128)} %bitcast.9) | data formatting | bytes 294912

commit v3 on v2

--- a/solution.py
+++ b/solution.py
@@ -20,9 +20,13 @@
 CSLOT = 72
 CHUNK = 4 * SLOT
 
-ORDER = [(0, 0), (1, 0), (-1, 0), (0, 1), (2, 0), (1, 1), (-1, 1), (2, 1)]
-PLANE = ORDER[1:]
-BACK = ORDER[::-1]
+SIDE = (1, -1)
+ACROSS = (1, -1, 2)
+PLANE = [(1, 0), (-1, 0), (2, 0), (0, 1), (2, 1)]
+GREET = PLANE + [(1, 1), (-1, 1)]
+ORDER = [(0, 0)] + PLANE + [(1, 1), (-1, 1)]
+BACK = [(1, 1), (-1, 1), (2, 0), (2, 1), (1, 0), (-1, 0), (0, 1), (0, 0)]
+QUEUE = BACK[2:]
 
 
 def place():
@@ -73,6 +77,10 @@
     def device(self, dp, r, dq):
         return at(*self.coords(dp, r, dq))
 
+    def beside(self, dp):
+        device = self.device(0, 1, 0)
+        return device if dp == 1 else {"dp": 1 - lax.axis_index("dp"), **device}
+
 
 def rel(dp, r, dq):
     return ((dp % 4) * 2 + r) * 4 + dq % 4
@@ -83,7 +91,7 @@
         self.a, self.buf, self.send, self.recv = axis, buf, send, recv
         self.copies = []
 
-    def put(self, dp, r, dq, to):
+    def put(self, dp, r, dq, to, device=None):
         tp, tr, tq = to
         a = self.a
         slot = a.slot(dp, r, dq)
@@ -92,7 +100,7 @@
             dst_ref=self.buf.at[slot],
             send_sem=self.send.at[len(self.copies)],
             recv_sem=self.recv.at[rel(dp - tp, (r + tr) % 2, dq - tq)],
-            device_id=a.device(tp, tr, tq),
+            device_id=a.device(tp, tr, tq) if device is None else device,
             device_id_type=MESH,
         )
         copy.start()
@@ -112,19 +120,28 @@
 
     def spread(self):
         for dp, r in PLANE:
-            self.put(0, 0, 0, (dp, r, 0))
-
-    def along(self, i):
-        dp, r = ORDER[i]
-        if i > 0:
+            self.put(0, 0, 0, (-dp, r, 0))
+
+    def along(self, dp, r):
+        if (dp, r) != (0, 0):
             self.await_(dp, r, 0)
-        for dq in (1, -1, 2):
+        for dq in ACROSS:
             self.put(dp, r, 0, (0, 0, dq))
-
-    def last(self, i):
-        dp, r = ORDER[i]
-        for dq in (1, -1, 2):
-            self.await_(dp, r, dq)
+        if r == 0 and dp in SIDE:
+            self.put(dp, 0, 0, (0, 1, 0), self.a.beside(dp))
+
+    def sideways(self, dq):
+        for dp in SIDE:
+            self.await_(dp, 0, dq)
+            self.put(dp, 0, dq, (0, 1, 0), self.a.beside(dp))
+
+    def last(self, dp, r):
+        if r == 1 and dp in SIDE:
+            for dq in (0,) + ACROSS:
+                self.await_(dp, r, dq)
+        elif r == 1 or dp not in SIDE:
+            for dq in ACROSS:
+                self.await_(dp, r, dq)
 
     def drain(self):
         for copy in self.copies:
@@ -140,8 +157,8 @@
 
 def partners():
     pa, pc = Axis(True), Axis(False)
-    return [pa.device(dp, r, 0) for dp, r in PLANE] + [
-        pc.device(dp, r, 0) for dp, r in PLANE if dp != 0
+    return [pa.device(dp, r, 0) for dp, r in GREET] + [
+        pc.device(dp, r, 0) for dp, r in GREET if dp != 0
     ]
 
 
@@ -196,34 +213,58 @@
         ).wait_recv()
         return self.got[k].astype(F32)
 
-    def part(self, dp, r, dq, i):
-        return self.own(self.a.slot(dp, r, dq), dq, i)
-
-    def first(self, i):
-        dp, r = BACK[i]
-        for j, dq in enumerate((2, 1, -1)):
-            value = None if self.placed else self.part(dp, r, dq, i)
-            self.put(3 * i + j, value, self.a.device(0, 0, dq))
-
-    def second(self, i):
-        dp, r = BACK[i]
-        total = self.part(dp, r, 0, i)
-        for j in range(3):
-            total = total + self.take(3 * i + j)
-        if i < 7:
-            self.put(24 + i, total, self.a.device(dp, r, 0))
+    def part(self, dp, r, dq):
+        return self.own(self.a.slot(dp, r, dq), dp, r, dq)
+
+    def summed(self, dp, r, dq):
+        value = self.part(dp, r, dq)
+        if r == 0 and dp in SIDE:
+            value = value + self.take(side_slot(dp, dq))
+        return value
+
+    def first(self, dp, r):
+        if r == 1 and dp in SIDE:
+            for dq in ACROSS + (0,):
+                value = None if self.placed else self.part(dp, r, dq)
+                self.put(side_slot(dp, dq), value, self.a.beside(dp))
         else:
+            ready = self.placed and not (r == 0 and dp in SIDE)
+            for dq in ACROSS:
+                value = None if ready else self.summed(dp, r, dq)
+                self.put(queue_slot(dp, r, dq), value, self.a.device(0, 0, dq))
+
+    def second(self, dp, r):
+        total = self.summed(dp, r, 0)
+        for dq in ACROSS:
+            total = total + self.take(queue_slot(dp, r, dq))
+        if (dp, r) == (0, 0):
             self.kept = total
+        else:
+            self.put(26 + PLANE.index((dp, r)), total, self.a.device(dp, r, 0))
 
     def third(self):
-        for i in range(7):
-            self.kept = self.kept + self.take(24 + i)
+        for i in range(len(PLANE)):
+            self.kept = self.kept + self.take(26 + i)
         self.put(31, self.kept, {"dp": 1 - lax.axis_index("dp")})
 
     def fourth(self):
         self.store(self.stage[31].astype(F32) + self.take(31))
         for copy in self.copies:
             copy.wait_send()
+
+
+def side_slot(dp, dq):
+    return SIDE.index(dp) * 4 + dq % 4
+
+
+def queue_slot(dp, r, dq):
+    return 8 + QUEUE.index((dp, r)) * 3 + ACROSS.index(dq)
+
+
+def part_slot(dp, r, dq):
+    if dq == 0:
+        return QUEUE.index((dp, r))
+    return 6 + SIDE.index(dp) * 3 + ACROSS.index(dq)
 
 
 def main_kernel(
@@ -310,7 +351,7 @@
     x1 = at(x + 1 - 2 * (x % 2), y, z)
     x2 = at((x + 2) % 4, y, z)
     y1 = at(x, 1 - y, z)
-    entry_barrier(partners() + [sibling, dp_peer, up_other, down_other])
+    entry_barrier(partners() + [sibling, dp_peer, up_other, down_other, pa.beside(-1)])
 
     gp = Gather(pa, wproj, psend, precv)
     gc = Gather(Axis(False), wconv, csend, crecv)
@@ -321,8 +362,8 @@
 
     gp.spread()
     gc.spread()
-    gp.along(0)
-    gc.along(0)
+    gp.along(0, 0)
+    gc.along(0, 0)
 
     yy = lax.broadcasted_iota(jnp.int32, (96, HALF), 0)
     nn = lax.broadcasted_iota(jnp.int32, (96, HALF), 1)
@@ -359,21 +400,22 @@
 
         lax.fori_loop(0, TOKENS // 256, step, 0)
 
-    for i in range(1, 8):
-        gp.along(i)
-        gc.along(i)
-        if i == 7:
-
-            @pl.when(seg == 0)
-            def _():
-                pl.semaphore_signal(gate, inc=1, device_id=sibling, device_id_type=MESH)
-
-        if i >= 2:
-            gp.last(i - 2)
-            gc.last(i - 2)
-            project(i - 2)
-    gc.last(6)
-    gc.last(7)
+    for dp, r in PLANE:
+        gp.along(dp, r)
+        gc.along(dp, r)
+    for dq in ACROSS:
+        gp.sideways(dq)
+        gc.sideways(dq)
+
+    @pl.when(seg == 0)
+    def _():
+        pl.semaphore_signal(gate, inc=1, device_id=sibling, device_id_type=MESH)
+
+    for i in range(6):
+        gp.last(*ORDER[i])
+        project(i)
+    for dp, r in ORDER:
+        gc.last(dp, r)
 
     def gather_rows(k, _):
         start = pl.multiple_of(k * CSLOT, 8)
@@ -390,10 +432,9 @@
         return 0
 
     lax.fori_loop(0, 9, to_bf, 0)
-    gp.last(6)
-    project(6)
-    gp.last(7)
-    project(7)
+    for i in (6, 7):
+        gp.last(*ORDER[i])
+        project(i)
 
     def flip_weights():
         def step(k, _):
@@ -645,12 +686,12 @@
     sum_end(2)
     sum_start(3)
 
-    def own_conv(slot, dq, i):
+    def own_conv(slot, dp, r, dq):
         start = pl.multiple_of(slot * CSLOT, 8)
         return wf32[:, pl.ds(start, CSLOT), :]
 
-    def own_proj(slot, dq, i):
-        return part[i]
+    def own_proj(slot, dp, r, dq):
+        return part[part_slot(dp, r, dq)]
 
     def store_conv(v):
         conv_out[...] = v
@@ -661,8 +702,7 @@
     rc = Reduce(Axis(False), own_conv, store_conv, wconv, cgot, rcs, rcr)
     rp = Reduce(pa, own_proj, store_proj, wproj, pgot, rps, rpr, placed=True)
 
-    def compute(i):
-        dp, r = BACK[i]
+    def compute(dp, r):
         xs, ys, _ = pa.coords(dp, r, 0)
         base = xs * 8 + ys * 4
         lanes = pl.ds(pl.multiple_of(base * SLOT, CHUNK), CHUNK)
@@ -670,27 +710,28 @@
         for k in range(4):
             ahead = (k - z + 4) % 4
             block = v[k * SLOT : (k + 1) * SLOT]
-            for dq, j in ((0, None), (2, 0), (1, 1), (3, 2)):
-
-                @pl.when(ahead == dq)
+            for dq in (0,) + ACROSS:
+
+                @pl.when(ahead == dq % 4)
                 def _():
-                    if j is None:
-                        part[i] = block
+                    if r == 1 and dp in SIDE:
+                        wproj[side_slot(dp, dq)] = block.astype(BF)
+                    elif dq == 0 or (r == 0 and dp in SIDE):
+                        part[part_slot(dp, r, dq)] = block
                     else:
-                        wproj[3 * i + j] = block.astype(BF)
-
-        rp.first(i)
-
-    for i in range(8):
-        rc.first(i)
-        compute(i)
+                        wproj[queue_slot(dp, r, dq)] = block.astype(BF)
+
+    for i, (dp, r) in enumerate(BACK):
+        rc.first(dp, r)
+        compute(dp, r)
+        rp.first(dp, r)
         if i in (1, 3, 5):
             sum_end(3 + i // 2)
             if i < 5:
                 sum_start(4 + i // 2)
-        if i >= 2:
-            rc.second(i - 2)
-            rp.second(i - 2)
+        if i >= 4:
+            rc.second(*BACK[i - 2])
+            rp.second(*BACK[i - 2])
     final = pltpu.make_async_remote_copy(
         src_ref=hsum.at[6],
         dst_ref=hfin,
@@ -705,9 +746,9 @@
         final.start()
         total_ref[...] = hsum[6]
 
-    for i in (6, 7):
-        rc.second(i)
-        rp.second(i)
+    for dp, r in BACK[6:]:
+        rc.second(dp, r)
+        rp.second(dp, r)
     rc.third()
     rp.third()
     rc.fourth()
@@ -769,7 +810,7 @@
             pltpu.VMEM((7, 8, CH), F32),
             pltpu.VMEM((6, 8, CH), F32),
             pltpu.VMEM((8, CH), F32),
-            pltpu.VMEM((8, SLOT, CH), F32),
+            pltpu.VMEM((12, SLOT, CH), F32),
             pltpu.VMEM((32, SLOT, CH), BF),
             pltpu.VMEM((32, 2, CSLOT, CH), BF),
             dma((8,)),
@@ -799,6 +840,29 @@
     )(hooks, proj, conv, head, light, illum, offsets, photos)
 
 
+def finish_kernel(npix, proj_ref, conv_ref, total_ref, proj_out, conv_out, head_out, loss_out):
+    proj_out[...] = proj_ref[...]
+    conv_out[...] = conv_ref[...]
+    head_out[...] = total_ref[0:3, :]
+    loss_out[...] = total_ref[3:4, 0:1] / npix
+
+
+def run_finish(npix, proj, conv, total):
+    vm = pl.BlockSpec(memory_space=pltpu.VMEM)
+    return pl.pallas_call(
+        functools.partial(finish_kernel, npix),
+        out_shape=(
+            jax.ShapeDtypeStruct((SLOT, CH), F32),
+            jax.ShapeDtypeStruct((2, CSLOT, CH), F32),
+            jax.ShapeDtypeStruct((3, CH), F32),
+            jax.ShapeDtypeStruct((1, 1), F32),
+        ),
+        in_specs=[vm, vm, vm],
+        out_specs=(vm, vm, vm, vm),
+        name="finish_kernel",
+    )(proj, conv, total)
+
+
 def body(hooks, proj_weight, conv_weight, head_weight, light_color, illum, offsets, photos):
     npix = 3 * MICROS * lax.axis_size("dp") * ROWS * lax.axis_size("fsdp") * COLS
     factor = 2.0 * LOSS_SCALE / npix
@@ -807,7 +871,8 @@
         factor, tokens, proj_weight[0], conv_weight[0], head_weight, light_color.T,
         illum, offsets.transpose(0, 2, 1), photos,
     )
-    return (grad_proj[None], grad_conv[None], total[:3], total[3, 0] / npix)
+    grad_proj, grad_conv, head, loss = run_finish(npix, grad_proj, grad_conv, total)
+    return (grad_proj[None], grad_conv[None], head, loss[0, 0])
 
 
 def solution(mesh):

time: 138 us -> 115 us (0.83)
  Pallas kernels: 130 us -> 114 us
  local copies, waits for them, and re-layouts: 5.67 us -> 0 us
  between operations: 2.43 us -> 0.64 us
    pallas_call x1, Pallas kernels: 130 us -> 112 us  [run_main(): pl.pallas_call(functools.partial(main_kernel, factor), out_shape=(jax.Sha...]
    unnamed x2 -> x0, local copies, waits for them, and re-layouts: 3.2 us -> none
    slice x2 -> x0, local copies, waits for them, and re-layouts: 2.47 us -> none  [body(): return (grad_proj[None], grad_conv[None], total[:3], total[3, 0] / npix)]
    pallas_call x0 -> x1, Pallas kernels: none -> 1.74 us  [run_finish(): pl.pallas_call(functools.partial(finish_kernel, npix), out_shape=(jax.Sha...]
where the time goes in v3:
time: 115 us
  Pallas kernels  114 us (99%)
    pallas_call x1, Pallas kernels, run_main(): pl.pallas_call(functools.partial(main_kernel, factor), out_shape=(jax.Sha...  112 us

profile of v3, /device:TPU:0, one launch (start us, length us, event | category | flops | bytes accessed | tf_op | source)
XLA Modules:
  0.0 114.5 jit_solution(12238995736047428053)
XLA Ops:
  0.6 112.1 %main_kernel.1 = (f32[192,256]{1,0:T(8,128)}, f32[2,72,256]{2,1,0:T(8,128)}, f32[8,256]{1,0:T(8,128)}) custom-call(bf16[1024,6144]{1,0:T(8,128)(2,1)} %bitcast.8, bf16[192,256]{1,0:T(8,128)(2,1)} %bitcast.11, bf16[2,72,256]{2,1,0:T(8,128)(2,1)} %bitcast.12, bf16[3,256]{1,0:T(4,128)(2,1)} %head_ref.1, f32[3,25]{1,0:T(4,128)} %bitcast.13, s32[2,4]{1,0:T(2,128)} %illum_ref.1, ...), custom_call_target="tpu_custom_call" | custom-call | flops 15000000512 | bytes 14000000 | tf_op jit(solution)/shard_map/main_kernel/pallas_call | solution.py:776
  112.8 1.7 %finish_kernel.1 = (f32[192,256]{1,0:T(8,128)}, f32[2,72,256]{2,1,0:T(8,128)}, f32[3,256]{1,0:T(4,128)}, f32[1,1]{1,0:T(1,128)}) custom-call(f32[192,256]{1,0:T(8,128)} %get-tuple-element.11.proj_ref, f32[2,72,256]{2,1,0:T(8,128)} %get-tuple-element.12.conv_ref, f32[8,256]{1,0:T(8,128)} %get-tuple-element.13.total_ref), custom_call_target="tpu_custom_call" | custom-call | tf_op jit(solution)/shard_map/finish_kernel/pallas_call | solution.py:852

commit v4 on v3

--- a/solution.py
+++ b/solution.py
@@ -174,10 +174,11 @@
 
 def shift_parts(v):
     n = v.shape[0]
-    col = lax.broadcasted_iota(jnp.int32, v.shape, 0) % COLS
-    before = jnp.where(col == 0, 0.0, pltpu.roll(v, 1, 0))
-    after = jnp.where(col == COLS - 1, 0.0, pltpu.roll(v, n - 1, 0))
-    return before.astype(BF), v.astype(BF), after.astype(BF)
+    grid = (n // COLS, COLS, CH)
+    col = lax.broadcasted_iota(jnp.int32, (1, COLS, CH), 1)
+    before = jnp.where(col == 0, 0.0, pltpu.roll(v, 1, 0).reshape(grid))
+    after = jnp.where(col == COLS - 1, 0.0, pltpu.roll(v, n - 1, 0).reshape(grid))
+    return before.astype(BF), v.reshape(grid).astype(BF), after.astype(BF)
 
 
 class Reduce:
@@ -281,6 +282,7 @@
     conv_out,
     total_ref,
     hooks_v,
+    photos_v,
     wproj,
     wconv,
     wf32,
@@ -341,6 +343,11 @@
 
     pa = Axis(True)
     loads = load_rows(hooks_ref, hooks_v, load_sem)
+    pictures = []
+    for m in range(MICROS):
+        copy = pltpu.make_async_copy(photos_ref.at[m, x], photos_v.at[m], load_sem.at[8 + m])
+        copy.start()
+        pictures.append(copy)
 
     me = x * 8 + y * 4 + z
     wproj[me] = proj_ref[...]
@@ -369,13 +376,14 @@
     nn = lax.broadcasted_iota(jnp.int32, (96, HALF), 1)
     row8 = lax.broadcasted_iota(jnp.int32, (8, HALF), 0)
     for m in range(MICROS):
+        pictures[m].wait()
         oy = offsets_ref[m, 0, x]
         ox = offsets_ref[m, 1, x]
         pick_col = (yy == ox + nn % COLS).astype(F32).astype(BF)
         pick_row = yy == oy + band * ROWS + nn // COLS
         block = jnp.zeros((8, HALF), F32)
         for c in range(3):
-            q = dot(photos_ref[m, x, c], pick_col)
+            q = dot(photos_v[m, c], pick_col)
             line = jnp.sum(jnp.where(pick_row, q, 0.0), axis=0, keepdims=True)
             block = jnp.where(row8 == c, line, block)
         targets[:, m * HALF : (m + 1) * HALF] = block
@@ -411,19 +419,22 @@
     def _():
         pl.semaphore_signal(gate, inc=1, device_id=sibling, device_id_type=MESH)
 
-    for i in range(6):
+    pc = gc.a
+
+    def gather_rows(dp, r):
+        for dq in (0,) + ACROSS:
+            k = pc.slot(dp, r, dq)
+            rows = pl.ds(pl.multiple_of(k * CSLOT, 8), CSLOT)
+            wf32[0, rows, :] = wconv[k, 0].astype(F32)
+            wf32[1, rows, :] = wconv[k, 1].astype(F32)
+
+    for i in range(7):
         gp.last(*ORDER[i])
         project(i)
-    for dp, r in ORDER:
-        gc.last(dp, r)
-
-    def gather_rows(k, _):
-        start = pl.multiple_of(k * CSLOT, 8)
-        wf32[0, pl.ds(start, CSLOT), :] = wconv[k, 0].astype(F32)
-        wf32[1, pl.ds(start, CSLOT), :] = wconv[k, 1].astype(F32)
-        return 0
-
-    lax.fori_loop(0, 32, gather_rows, 0)
+        gc.last(*ORDER[i])
+        gather_rows(*ORDER[i])
+    gc.last(*ORDER[7])
+    gather_rows(*ORDER[7])
 
     def to_bf(k, _):
         start = pl.multiple_of(k * CH, CH)
@@ -432,9 +443,8 @@
         return 0
 
     lax.fori_loop(0, 9, to_bf, 0)
-    for i in (6, 7):
-        gp.last(*ORDER[i])
-        project(i)
+    gp.last(*ORDER[7])
+    project(7)
 
     def flip_weights():
         def step(k, _):
@@ -486,9 +496,9 @@
     def fill(cat, m, row, value):
         a, b, c = shift_parts(value)
         n = value.shape[0] // COLS
-        cat[m, row : row + n, :, 0:CH] = a.reshape(n, COLS, CH)
-        cat[m, row : row + n, :, CH : 2 * CH] = b.reshape(n, COLS, CH)
-        cat[m, row : row + n, :, 2 * CH : 3 * CH] = c.reshape(n, COLS, CH)
+        cat[m, row : row + n, :, 0:CH] = a
+        cat[m, row : row + n, :, CH : 2 * CH] = b
+        cat[m, row : row + n, :, 2 * CH : 3 * CH] = c
 
     def tokens_of(m):
         return slice(m * HALF, (m + 1) * HALF)
@@ -675,16 +685,9 @@
         edges(3, grad)
         halo_start(3, up_other, down_other)
         seg_copy(grad, og_in, 1).start()
-        transposes()
 
     sum_end(0)
     sum_start(1)
-    conv_weight_grad(x2t, cat_c, 3, 1)
-    sum_end(1)
-    sum_start(2)
-    conv_weight_grad(x1t, cat_d, 2, 0)
-    sum_end(2)
-    sum_start(3)
 
     def own_conv(slot, dp, r, dq):
         start = pl.multiple_of(slot * CSLOT, 8)
@@ -722,13 +725,24 @@
                         wproj[queue_slot(dp, r, dq)] = block.astype(BF)
 
     for i, (dp, r) in enumerate(BACK):
-        rc.first(dp, r)
         compute(dp, r)
         rp.first(dp, r)
-        if i in (1, 3, 5):
-            sum_end(3 + i // 2)
-            if i < 5:
-                sum_start(4 + i // 2)
+        if i == 2:
+
+            @pl.when(seg == 1)
+            def _():
+                transposes()
+
+            conv_weight_grad(x2t, cat_c, 3, 1)
+            conv_weight_grad(x1t, cat_d, 2, 0)
+            rc.first(*BACK[0])
+            rc.first(*BACK[1])
+        if i >= 2:
+            rc.first(dp, r)
+            if i < 7:
+                sum_end(i - 1)
+                if i < 6:
+                    sum_start(i)
         if i >= 4:
             rc.second(*BACK[i - 2])
             rp.second(*BACK[i - 2])
@@ -780,10 +794,11 @@
             jax.ShapeDtypeStruct((2, CSLOT, CH), F32),
             jax.ShapeDtypeStruct((8, CH), F32),
         ),
-        in_specs=[pl.BlockSpec(memory_space=pl.ANY), vm, vm, vm, sm, sm, sm, vm],
+        in_specs=[pl.BlockSpec(memory_space=pl.ANY), vm, vm, vm, sm, sm, sm, pl.BlockSpec(memory_space=pl.ANY)],
         out_specs=(vm, vm, vm),
         scratch_shapes=[
             pltpu.VMEM((TOKENS, D), BF),
+            pltpu.VMEM((MICROS, 3, 96, 96), BF),
             pltpu.VMEM((32, SLOT, CH), BF),
             pltpu.VMEM((32, 2, CSLOT, CH), BF),
             pltpu.VMEM((2, 9 * CH, CH), F32),
@@ -813,7 +828,7 @@
             pltpu.VMEM((12, SLOT, CH), F32),
             pltpu.VMEM((32, SLOT, CH), BF),
             pltpu.VMEM((32, 2, CSLOT, CH), BF),
-            dma((8,)),
+            dma((8 + MICROS,)),
             dma((32,)),
             dma((32,)),
             dma((32,)),

time: 115 us -> 111 us (0.965)
  Pallas kernels: 114 us -> 110 us
    pallas_call x1, Pallas kernels: 112 us -> 108 us  [run_main(): pl.pallas_call(functools.partial(main_kernel, factor), out_shape=(jax.Sha...]
where the time goes in v4:
time: 111 us
  Pallas kernels  110 us (99%)
    pallas_call x1, Pallas kernels, run_main(): pl.pallas_call(functools.partial(main_kernel, factor), out_shape=(jax.Sha...  108 us

profile of v4, /device:TPU:0, one launch (start us, length us, event | category | flops | bytes accessed | tf_op | source)
XLA Modules:
  0.0 110.9 jit_solution(2953594520662761054)
XLA Ops:
  0.6 108.5 %main_kernel.1 = (f32[192,256]{1,0:T(8,128)}, f32[2,72,256]{2,1,0:T(8,128)}, f32[8,256]{1,0:T(8,128)}) custom-call(bf16[1024,6144]{1,0:T(8,128)(2,1)} %bitcast.8, bf16[192,256]{1,0:T(8,128)(2,1)} %bitcast.11, bf16[2,72,256]{2,1,0:T(8,128)(2,1)} %bitcast.12, bf16[3,256]{1,0:T(4,128)(2,1)} %head_ref.1, f32[3,25]{1,0:T(4,128)} %bitcast.13, s32[2,4]{1,0:T(2,128)} %illum_ref.1, ...), custom_call_target="tpu_custom_call" | custom-call | flops 15000000512 | bytes 14000000 | tf_op jit(solution)/shard_map/main_kernel/pallas_call | solution.py:790
  109.1 1.7 %finish_kernel.1 = (f32[192,256]{1,0:T(8,128)}, f32[2,72,256]{2,1,0:T(8,128)}, f32[3,256]{1,0:T(4,128)}, f32[1,1]{1,0:T(1,128)}) custom-call(f32[192,256]{1,0:T(8,128)} %get-tuple-element.11.proj_ref, f32[2,72,256]{2,1,0:T(8,128)} %get-tuple-element.12.conv_ref, f32[8,256]{1,0:T(8,128)} %get-tuple-element.13.total_ref), custom_call_target="tpu_custom_call" | custom-call | tf_op jit(solution)/shard_map/finish_kernel/pallas_call | solution.py:867

commit v5 on v4

--- a/solution.py
+++ b/solution.py
@@ -25,8 +25,8 @@
 PLANE = [(1, 0), (-1, 0), (2, 0), (0, 1), (2, 1)]
 GREET = PLANE + [(1, 1), (-1, 1)]
 ORDER = [(0, 0)] + PLANE + [(1, 1), (-1, 1)]
-BACK = [(1, 1), (-1, 1), (2, 0), (2, 1), (1, 0), (-1, 0), (0, 1), (0, 0)]
-QUEUE = BACK[2:]
+BACK = [(2, 0), (1, 1), (-1, 1), (2, 1), (1, 0), (-1, 0), (0, 1), (0, 0)]
+QUEUE = [BACK[0]] + BACK[3:]
 
 
 def place():
@@ -76,6 +76,12 @@
 
     def device(self, dp, r, dq):
         return at(*self.coords(dp, r, dq))
+
+    def fellow(self, dp, r):
+        device = self.device(dp, r, 0)
+        if (dp, r) == (2, 1):
+            device = {"dp": 1 - lax.axis_index("dp"), **device}
+        return device
 
     def beside(self, dp):
         device = self.device(0, 1, 0)
@@ -120,7 +126,7 @@
 
     def spread(self):
         for dp, r in PLANE:
-            self.put(0, 0, 0, (-dp, r, 0))
+            self.put(0, 0, 0, (-dp, r, 0), self.a.fellow(-dp if dp != 2 else 2, r))
 
     def along(self, dp, r):
         if (dp, r) != (0, 0):
@@ -241,7 +247,7 @@
         if (dp, r) == (0, 0):
             self.kept = total
         else:
-            self.put(26 + PLANE.index((dp, r)), total, self.a.device(dp, r, 0))
+            self.put(26 + PLANE.index((dp, r)), total, self.a.fellow(dp, r))
 
     def third(self):
         for i in range(len(PLANE)):
@@ -358,7 +364,11 @@
     x1 = at(x + 1 - 2 * (x % 2), y, z)
     x2 = at((x + 2) % 4, y, z)
     y1 = at(x, 1 - y, z)
-    entry_barrier(partners() + [sibling, dp_peer, up_other, down_other, pa.beside(-1)])
+    entry_barrier(
+        partners()
+        + [sibling, dp_peer, up_other, down_other, pa.beside(-1)]
+        + [pa.fellow(2, 1), Axis(False).fellow(2, 1)]
+    )
 
     gp = Gather(pa, wproj, psend, precv)
     gc = Gather(Axis(False), wconv, csend, crecv)
@@ -743,9 +753,9 @@
                 sum_end(i - 1)
                 if i < 6:
                     sum_start(i)
-        if i >= 4:
-            rc.second(*BACK[i - 2])
-            rp.second(*BACK[i - 2])
+        if i >= 5:
+            rc.second(*QUEUE[i - 5])
+            rp.second(*QUEUE[i - 5])
     final = pltpu.make_async_remote_copy(
         src_ref=hsum.at[6],
         dst_ref=hfin,
@@ -760,7 +770,7 @@
         final.start()
         total_ref[...] = hsum[6]
 
-    for dp, r in BACK[6:]:
+    for dp, r in QUEUE[3:]:
         rc.second(dp, r)
         rp.second(dp, r)
     rc.third()

time: 111 us -> 111 us (level)
  no operation moved by 1% of the time
where the time goes in v5:
time: 111 us; the launch traced here: 110 us
  Pallas kernels  110 us (99%)
    pallas_call x1, Pallas kernels, run_main(): pl.pallas_call(functools.partial(main_kernel, factor), out_shape=(jax.Sha...  108 us

profile of v5, /device:TPU:0, one launch (start us, length us, event | category | flops | bytes accessed | tf_op | source)
XLA Modules:
  0.0 110.4 jit_solution(17859340373729603096)
XLA Ops:
  0.6 108.0 %main_kernel.1 = (f32[192,256]{1,0:T(8,128)}, f32[2,72,256]{2,1,0:T(8,128)}, f32[8,256]{1,0:T(8,128)}) custom-call(bf16[1024,6144]{1,0:T(8,128)(2,1)} %bitcast.8, bf16[192,256]{1,0:T(8,128)(2,1)} %bitcast.11, bf16[2,72,256]{2,1,0:T(8,128)(2,1)} %bitcast.12, bf16[3,256]{1,0:T(4,128)(2,1)} %head_ref.1, f32[3,25]{1,0:T(4,128)} %bitcast.13, s32[2,4]{1,0:T(2,128)} %illum_ref.1, ...), custom_call_target="tpu_custom_call" | custom-call | flops 15000000512 | bytes 14000000 | tf_op jit(solution)/shard_map/main_kernel/pallas_call | solution.py:800
  108.7 1.7 %finish_kernel.1 = (f32[192,256]{1,0:T(8,128)}, f32[2,72,256]{2,1,0:T(8,128)}, f32[3,256]{1,0:T(4,128)}, f32[1,1]{1,0:T(1,128)}) custom-call(f32[192,256]{1,0:T(8,128)} %get-tuple-element.11.proj_ref, f32[2,72,256]{2,1,0:T(8,128)} %get-tuple-element.12.conv_ref, f32[8,256]{1,0:T(8,128)} %get-tuple-element.13.total_ref), custom_call_target="tpu_custom_call" | custom-call | tf_op jit(solution)/shard_map/finish_kernel/pallas_call | solution.py:877

commit v6 on v5

--- a/solution.py
+++ b/solution.py
@@ -21,7 +21,7 @@
 CHUNK = 4 * SLOT
 
 SIDE = (1, -1)
-ACROSS = (1, -1, 2)
+ACROSS = (2, 1, -1)
 PLANE = [(1, 0), (-1, 0), (2, 0), (0, 1), (2, 1)]
 GREET = PLANE + [(1, 1), (-1, 1)]
 ORDER = [(0, 0)] + PLANE + [(1, 1), (-1, 1)]
@@ -421,7 +421,7 @@
     for dp, r in PLANE:
         gp.along(dp, r)
         gc.along(dp, r)
-    for dq in ACROSS:
+    for dq in (1, -1, 2):
         gp.sideways(dq)
         gc.sideways(dq)
 

time: 111 us -> 111 us (level)
  no operation moved by 1% of the time
where the time goes in v6:
time: 111 us; the launch traced here: 110 us
  Pallas kernels  110 us (99%)
    pallas_call x1, Pallas kernels, run_main(): pl.pallas_call(functools.partial(main_kernel, factor), out_shape=(jax.Sha...  108 us

profile of v6, /device:TPU:0, one launch (start us, length us, event | category | flops | bytes accessed | tf_op | source)
XLA Modules:
  0.0 110.4 jit_solution(15861326592531978911)
XLA Ops:
  0.6 108.0 %main_kernel.1 = (f32[192,256]{1,0:T(8,128)}, f32[2,72,256]{2,1,0:T(8,128)}, f32[8,256]{1,0:T(8,128)}) custom-call(bf16[1024,6144]{1,0:T(8,128)(2,1)} %bitcast.8, bf16[192,256]{1,0:T(8,128)(2,1)} %bitcast.11, bf16[2,72,256]{2,1,0:T(8,128)(2,1)} %bitcast.12, bf16[3,256]{1,0:T(4,128)(2,1)} %head_ref.1, f32[3,25]{1,0:T(4,128)} %bitcast.13, s32[2,4]{1,0:T(2,128)} %illum_ref.1, ...), custom_call_target="tpu_custom_call" | custom-call | flops 15000000512 | bytes 14000000 | tf_op jit(solution)/shard_map/main_kernel/pallas_call | solution.py:800
  108.6 1.7 %finish_kernel.1 = (f32[192,256]{1,0:T(8,128)}, f32[2,72,256]{2,1,0:T(8,128)}, f32[3,256]{1,0:T(4,128)}, f32[1,1]{1,0:T(1,128)}) custom-call(f32[192,256]{1,0:T(8,128)} %get-tuple-element.11.proj_ref, f32[2,72,256]{2,1,0:T(8,128)} %get-tuple-element.12.conv_ref, f32[8,256]{1,0:T(8,128)} %get-tuple-element.13.total_ref), custom_call_target="tpu_custom_call" | custom-call | tf_op jit(solution)/shard_map/finish_kernel/pallas_call | solution.py:877
